TPU v7x, 256 devices: a whole 4x4x8 slice. The times are simulated.
256 devices in a mesh: member: 32 (over y, x, core), head: 8 (over z).
Axes of the slice: x: 4, y: 4, z: 8, core: 2. Of those that a mesh axis runs over, the one named last changes fastest.
Arguments:
- hidden: bfloat16 [32, 32, 16, 2880], P('member', 'head'), may hold values from -6 to 6
- joined_weight: bfloat16 [2880, 8, 640], P(None, 'head'), may hold values from -0.109375 to 0.109375
- output_weight: bfloat16 [4096, 2880], P('head'), may hold values from -0.09375 to 0.09375
- key_cache: bfloat16 [32, 8, 16, 65536], P('member', 'head'), may hold values from -330 to 330
- value_cache: bfloat16 [32, 8, 16, 65536], P('member', 'head'), may hold values from -8 to 8
- sink_logits: float32 [64], P('head'), may hold values from 3 to 10
- lengths: int32 [32, 16], P('member'), may hold values from 2 to 1024, as said below
- query_left: float32 [32, 4, 2880], P('member'), may hold values from -6 to 6
- query_right: float32 [32, 4, 4096], P('member', None, 'head'), may hold values from -6 to 6
- output_left: float32 [32, 4, 4096], P('member', None, 'head'), may hold values from -6 to 6
- output_right: float32 [32, 4, 2880], P('member'), may hold values from -6 to 6
- fitness: float32 [32], P('member'), may hold values from -4 to 4
- query_master: float32 [2880, 4096], P('member', 'head'), may hold values from -6 to 6
- query_moment: float32 [2880, 4096], P('member', 'head'), may hold values from -2 to 2
- output_master: float32 [2880, 4096], P('member', 'head'), may hold values from -6 to 6
- output_moment: float32 [2880, 4096], P('member', 'head'), may hold values from -2 to 2
Outputs:
- layer_output: bfloat16 [32, 32, 16, 2880], P('member', 'head')
- query_weights: float32 [2880, 4096], P('member', 'head')
- query_momenta: float32 [2880, 4096], P('member', 'head')
- output_weights: float32 [2880, 4096], P('member', 'head')
- output_momenta: float32 [2880, 4096], P('member', 'head')
Inputs may be any that keep to these rules, and one draw needn't show every extreme that they name: `lengths`: in every member one sequence has all 1024 slots filled.
All inputs are finite; a program needn't handle non-finite values.
Results may differ from a plain program's by a relative error of at most 0.012.
Values may be sent and summed in bfloat16 or wider, within the bound.
No kernel may reach another device: no remote copies, remote signals or barrier semaphores. Data moves between devices by JAX's collectives and lax.ppermute only.
A program may use at most 128 MiB of HBM per device.

v0:
```python
import functools
import math

import jax
import jax.numpy as jnp
from jax import lax
from jax.experimental import pallas as pl
from jax.experimental.pallas import tpu as pltpu
from jax.sharding import PartitionSpec as P

D = 2880
HEAD_DIM = 64
QDIM = 4096
LANES = 128

rotary_base = 150000.0
noise_scale = 0.5
moment_decay = 0.9
learn_rate = 0.2
masked_score = -1e30


RELAYOUT_PARTS = 8


def relayout_kernel(key_hbm, value_hbm, key_out, value_out, held, made, scratch, in_sems, out_sems):
    rows, width = key_hbm.shape
    part = width // RELAYOUT_PARTS
    tiles = part // LANES
    arrays = ((key_hbm, key_out), (value_hbm, value_out))

    def copy_in(a, i):
        at = pl.ds(i * part, part)
        return pltpu.make_async_copy(
            arrays[a][0].at[:, at], held.at[a, :, at], in_sems.at[a * RELAYOUT_PARTS + i]
        )

    def copy_out(a, i):
        at = pl.ds(i * tiles, tiles)
        return pltpu.make_async_copy(
            made.at[a, :, at, :], arrays[a][1].at[:, at, :], out_sems.at[a * RELAYOUT_PARTS + i]
        )

    steps = [(a, i) for a in range(2) for i in range(RELAYOUT_PARTS)]
    for a, i in steps:
        copy_in(a, i).start()
    for a, i in steps:
        copy_in(a, i).wait()
        for t in range(tiles):
            at = i * part + t * LANES
            scratch[a, t * rows : (t + 1) * rows, :] = held[a, :, at : at + LANES].astype(
                jnp.float32
            )
        for b in range(rows):
            made[a, b, i * tiles : (i + 1) * tiles, :] = scratch[
                a, pl.ds(b, tiles, stride=rows), :
            ].astype(jnp.bfloat16)
        copy_out(a, i).start()
    for a, i in steps:
        copy_out(a, i).wait()


def relayout(keys, values):
    rows, width = keys.shape
    out = jax.ShapeDtypeStruct((rows, width // LANES, LANES), keys.dtype)
    hbm = pl.BlockSpec(memory_space=pltpu.HBM)
    return pl.pallas_call(
        relayout_kernel,
        in_specs=[hbm] * 2,
        out_specs=[hbm] * 2,
        out_shape=[out, out],
        scratch_shapes=[
            pltpu.VMEM((2, rows, width), keys.dtype),
            pltpu.VMEM((2, rows, width // LANES, LANES), keys.dtype),
            pltpu.VMEM((2, rows * width // LANES // RELAYOUT_PARTS, LANES), jnp.float32),
            pltpu.SemaphoreType.DMA((2 * RELAYOUT_PARTS,)),
            pltpu.SemaphoreType.DMA((2 * RELAYOUT_PARTS,)),
        ],
        compiler_params=pltpu.CompilerParams(vmem_limit_bytes=60 * 1024 * 1024),
    )(keys, values)


def pack_kernel(fitness_ref, query_left, output_right, query_right, output_left, out_ref):
    score = fitness_ref[0]
    columns = query_right.shape[1]
    right = jnp.concatenate([query_right[...], output_left[...]], axis=0) * score
    left = jnp.concatenate([query_left[...], output_right[...]], axis=0)
    out_ref[:, :columns] = right.astype(jnp.bfloat16)
    pad = jnp.zeros((left.shape[0], out_ref.shape[1] - columns - left.shape[1]), jnp.float32)
    out_ref[:, columns:] = jnp.concatenate([left, pad], axis=1).astype(jnp.bfloat16)


def pack(fitness, query_left, output_right, query_right, output_left):
    rank, width = query_left.shape
    columns = query_right.shape[1]
    vmem = pl.BlockSpec(memory_space=pltpu.VMEM)
    return pl.pallas_call(
        pack_kernel,
        in_specs=[pl.BlockSpec(memory_space=pltpu.SMEM)] + [vmem] * 4,
        out_specs=vmem,
        out_shape=jax.ShapeDtypeStruct(
            (2 * rank, columns + pl.cdiv(width, LANES) * LANES), jnp.bfloat16
        ),
    )(fitness, query_left, output_right, query_right, output_left)


def update_kernel(
    start_ref,
    first_ref,
    second_ref,
    query_moment,
    query_master,
    output_moment,
    output_master,
    query_weights,
    query_momenta,
    output_weights,
    output_momenta,
    *,
    rank,
    member_count,
):
    share, columns = query_moment.shape
    start = start_ref[0]
    aligned = pl.multiple_of((start >> 7) << 7, LANES)
    shift = (2 * LANES - (start - aligned)) & (2 * LANES - 1)
    terms = []
    for ref in (first_ref, second_ref):
        left = ref[:, pl.ds(aligned, 2 * LANES)].astype(jnp.float32)
        left = pltpu.roll(left, shift, 1)[:, :LANES]
        row = lax.broadcasted_iota(jnp.int32, left.shape, 0)
        of_query = (row & (2 * rank - 1)) < rank
        for kind, chosen in enumerate((of_query, jnp.logical_not(of_query))):
            terms.append(
                lax.dot_general(
                    jnp.where(chosen, left, 0.0).astype(jnp.bfloat16),
                    ref[:, :columns],
                    (((0,), (0,)), ((), ())),
                    preferred_element_type=jnp.float32,
                )
            )
    for kind, (moment, master, weights, momenta) in enumerate(
        (
            (query_moment, query_master, query_weights, query_momenta),
            (output_moment, output_master, output_weights, output_momenta),
        )
    ):
        step = (terms[kind] + terms[2 + kind])[:share] / member_count
        new = moment_decay * moment[...] + step
        momenta[...] = new
        weights[...] = master[...] + learn_rate * new


def update(start, first, second, rank, member_count, *states):
    vmem = pl.BlockSpec(memory_space=pltpu.VMEM)

    def kernel(*refs):
        update_kernel(*refs, rank=rank, member_count=member_count)

    return pl.pallas_call(
        kernel,
        in_specs=[pl.BlockSpec(memory_space=pltpu.SMEM)] + [vmem] * 6,
        out_specs=[vmem] * 4,
        out_shape=[jax.ShapeDtypeStruct(states[0].shape, jnp.float32)] * 4,
        compiler_params=pltpu.CompilerParams(vmem_limit_bytes=16 * 1024 * 1024),
    )(start, first, second, *states)


def left_rows(left):
    hi = left.astype(jnp.bfloat16).astype(jnp.float32)
    lo = left - hi
    zeros = jnp.zeros((LANES - 24, left.shape[1]), jnp.float32)
    return jnp.concatenate([hi, hi, hi, lo, lo, lo, zeros], axis=0).astype(jnp.bfloat16)


def right_rows(right, scale):
    scaled = right * scale
    hi = scaled.astype(jnp.bfloat16).astype(jnp.float32)
    lo = scaled - hi
    zeros = jnp.zeros((LANES - 12, right.shape[1]), jnp.float32)
    return jnp.concatenate([hi, hi, lo, zeros], axis=0).astype(jnp.bfloat16)


def low_rank_operand(low):
    low = low + pltpu.roll(low, LANES - 12, 1)
    lane = lax.broadcasted_iota(jnp.int32, low.shape, 1)
    hi = low.astype(jnp.bfloat16).astype(jnp.float32)
    lo = low - hi
    return jnp.where((lane >= 4) & (lane < 8), lo, hi).astype(jnp.bfloat16)


CONTRACT_LAST = (((1,), (1,)), ((), ()))


def project(tokens, weight_wait, weight_ref, left_q, right_q, cosines, sines, store):
    qdim = right_q.shape[1]
    tiles = qdim // LANES
    low = lax.dot_general(
        tokens, left_rows(left_q), CONTRACT_LAST, preferred_element_type=jnp.float32
    )
    low = low_rank_operand(low)
    right = right_rows(right_q, noise_scale / math.sqrt(D))
    extra = jnp.dot(low, right, preferred_element_type=jnp.float32)
    lane = lax.broadcasted_iota(jnp.int32, cosines.shape, 1)
    first_half = (lane & (HEAD_DIM - 1)) < HEAD_DIM // 2

    def rotated(t):
        swapped = jnp.where(
            first_half,
            pltpu.roll(t, LANES - HEAD_DIM // 2, 1),
            pltpu.roll(t, HEAD_DIM // 2, 1),
        )
        return t * cosines + swapped * sines

    weight_wait()
    proj = jnp.dot(tokens, weight_ref[...], preferred_element_type=jnp.float32)
    for j in range(tiles):
        part = slice(j * LANES, (j + 1) * LANES)
        store(j, rotated(proj[:, part] + extra[:, part]) * (HEAD_DIM**-0.5))
    tail = proj[:, qdim:]
    store(tiles, jnp.where(lane < HEAD_DIM, rotated(tail), tail))


def project_kernel(*refs, chunk_count, first_row):
    chunks = refs[:chunk_count]
    weight_hbm, left_q_ref, right_q_ref, cos_ref, sin_ref, out_ref = refs[
        chunk_count : chunk_count + 6
    ]
    token_ref, weight_ref, sems = refs[chunk_count + 6 :]
    chunk_rows = chunks[0].shape[0]
    rows = chunk_rows * chunk_count
    copies = [
        pltpu.make_async_copy(
            chunks[c], token_ref.at[pl.ds(c * chunk_rows, chunk_rows)], sems.at[c]
        )
        for c in range(chunk_count)
    ]
    weight_copy = pltpu.make_async_copy(weight_hbm, weight_ref, sems.at[chunk_count])
    for copy in copies + [weight_copy]:
        copy.start()
    for copy in copies:
        copy.wait()
    here = pl.ds(first_row, rows)

    def store(j, value):
        out_ref[j] = value

    project(
        token_ref[...],
        weight_copy.wait,
        weight_ref,
        left_q_ref[...],
        right_q_ref[...],
        cos_ref[here, :],
        sin_ref[here, :],
        store,
    )


def project_chunks(chunks, first_row, weight, left_q, right_q, cosines, sines):
    chunk_rows, width = chunks[0].shape
    rows = chunk_rows * len(chunks)
    vmem = pl.BlockSpec(memory_space=pltpu.VMEM)
    either = pl.BlockSpec(memory_space=pl.ANY)

    def kernel(*refs):
        project_kernel(*refs, chunk_count=len(chunks), first_row=first_row)

    return pl.pallas_call(
        kernel,
        in_specs=[either] * (len(chunks) + 1) + [vmem] * 4,
        out_specs=vmem,
        out_shape=jax.ShapeDtypeStruct((weight.shape[1] // LANES, rows, LANES), jnp.float32),
        scratch_shapes=[
            pltpu.VMEM((rows, width), jnp.bfloat16),
            pltpu.VMEM(weight.shape, jnp.bfloat16),
            pltpu.SemaphoreType.DMA((len(chunks) + 1,)),
        ],
        compiler_params=pltpu.CompilerParams(vmem_limit_bytes=57 * 1024 * 1024),
    )(*chunks, weight, left_q, right_q, cosines, sines)


TOGETHER = 2


def layer_kernel(lengths_ref, sink_ref, place_ref, *refs, chunk_count, ready_count, own_steps):
    chunks = refs[:chunk_count]
    ready = refs[chunk_count : chunk_count + ready_count]
    refs = refs[chunk_count + ready_count :]
    (
        weight_hbm,
        out_weight_hbm,
        key_hbm,
        value_hbm,
        left_q_ref,
        right_q_ref,
        left_o_ref,
        right_o_ref,
        cos_ref,
        sin_ref,
    ) = refs[:10]
    (
        token_ref,
        weight_ref,
        out_weight_ref,
        key_ref,
        value_ref,
        proj_ref,
        att_ref,
        right_ref,
        bias_ref,
        sems,
        chunk_sems,
    ) = refs[-11:]
    outs = refs[10:-11]
    chunk_rows, width = chunks[0].shape
    copies = [
        pltpu.make_async_copy(
            chunks[c], token_ref.at[pl.ds(c * chunk_rows, chunk_rows)], chunk_sems.at[c]
        )
        for c in range(chunk_count)
    ]
    weight_copy = pltpu.make_async_copy(weight_hbm, weight_ref, sems.at[0])
    key_copy = pltpu.make_async_copy(key_hbm, key_ref, sems.at[1])
    value_copy = pltpu.make_async_copy(value_hbm, value_ref, sems.at[2])
    out_weight_copy = pltpu.make_async_copy(out_weight_hbm, out_weight_ref, sems.at[3])
    ready_copies = []
    first_row = 0
    for i in range(ready_count):
        count = ready[i].shape[1]
        ready_copies.append(
            pltpu.make_async_copy(
                ready[i], proj_ref.at[:, pl.ds(first_row, count), :], chunk_sems.at[chunk_count + i]
            )
        )
        first_row += count
    for copy in copies + [weight_copy] + ready_copies + [key_copy, value_copy, out_weight_copy]:
        copy.start()

    seqs = key_ref.shape[0]
    total_rows = proj_ref.shape[1]
    steps = total_rows // seqs
    qdim = right_q_ref.shape[1]
    group = qdim // HEAD_DIM
    tiles = qdim // LANES
    pairs = key_ref.shape[1]
    rows = group * steps

    right_ref[...] = right_rows(right_o_ref[...], noise_scale / math.sqrt(QDIM))
    for copy in copies:
        copy.wait()
    here = pl.ds(first_row, chunk_count * chunk_rows)

    def store(j, value):
        proj_ref[j, here, :] = value

    project(
        token_ref[...],
        weight_copy.wait,
        weight_ref,
        left_q_ref[...],
        right_q_ref[...],
        cos_ref[here, :],
        sin_ref[here, :],
        store,
    )

    ring = steps // own_steps
    place = place_ref[0]

    def step_of(dim):
        total = jnp.zeros((steps, steps), jnp.int32)
        row = lax.broadcasted_iota(jnp.int32, (steps, steps), dim)
        for order in range(ring):
            distance = (order + 1) // 2
            chunk = (place + ring + (distance if order % 2 else -distance)) & (ring - 1)
            at = order * own_steps
            total = jnp.where(row >= at, chunk * own_steps + row - at, total)
        return total

    bias = jnp.where(step_of(1) <= step_of(0), 0.0, masked_score)
    column = lax.broadcasted_iota(jnp.int32, (steps, LANES - steps), 1)
    for g in range(group):
        bias_ref[g * steps : (g + 1) * steps, :] = jnp.concatenate(
            [bias, jnp.where(column == 0, sink_ref[g], masked_score)], axis=1
        )
    pair = lax.broadcasted_iota(jnp.int32, (1, pairs), 1)
    low_lanes = lax.broadcasted_iota(jnp.int32, (steps, LANES), 1) < HEAD_DIM

    def several(i, carry):
        members = [i * TOGETHER + u for u in range(TOGETHER)]
        evens, odds, news, scored = [], [], [], []
        for b in members:
            even, odd = [], []
            for j in range(tiles):
                t = proj_ref[j, pl.ds(b, steps, stride=seqs), :]
                r = pltpu.roll(t, HEAD_DIM, 1)
                even += [jnp.where(low_lanes, t, 0.0), jnp.where(low_lanes, r, 0.0)]
                odd += [jnp.where(low_lanes, 0.0, r), jnp.where(low_lanes, 0.0, t)]
            evens.append(jnp.concatenate(even, axis=0).astype(jnp.bfloat16))
            odds.append(jnp.concatenate(odd, axis=0).astype(jnp.bfloat16))
            new_pair = proj_ref[tiles, pl.ds(b, steps, stride=seqs), :]
            nothing = jnp.zeros((LANES - steps, LANES), jnp.float32)
            news.append(jnp.concatenate([new_pair, nothing], axis=0).astype(jnp.bfloat16))
        for u, b in enumerate(members):
            length = lengths_ref[b]
            keys = key_ref[b]

            def scores(query, parity):
                valid = jnp.where(2 * pair + parity < length, 0.0, masked_score)
                return (
                    lax.dot_general(
                        query, keys, CONTRACT_LAST, preferred_element_type=jnp.float32
                    )
                    + valid
                )

            s_new = (
                lax.dot_general(
                    evens[u], news[u], CONTRACT_LAST, preferred_element_type=jnp.float32
                )
                + bias_ref[...]
            )
            scored.append((scores(evens[u], 0), scores(odds[u], 1), s_new))
        for u, b in enumerate(members):
            s_even, s_odd, s_new = scored[u]
            values = value_ref[b]

            def folded(join, even, odd, new):
                return functools.reduce(
                    join,
                    [x[:, i : i + LANES] for x in (even, odd) for i in range(0, pairs, LANES)],
                    new,
                )

            top = jnp.max(folded(jnp.maximum, s_even, s_odd, s_new), axis=1, keepdims=True)
            p_even = jnp.exp(s_even - top)
            p_odd = jnp.exp(s_odd - top)
            p_new = jnp.exp(s_new - top)
            total = jnp.sum(folded(jnp.add, p_even, p_odd, p_new), axis=1, keepdims=True)
            a_even = jnp.dot(
                p_even.astype(jnp.bfloat16), values, preferred_element_type=jnp.float32
            )
            a_odd = jnp.dot(
                p_odd.astype(jnp.bfloat16), values, preferred_element_type=jnp.float32
            ) + jnp.dot(p_new.astype(jnp.bfloat16), news[u], preferred_element_type=jnp.float32)
            inverse = 1.0 / total
            a_even = a_even * inverse
            a_odd = a_odd * inverse
            for j in range(tiles):
                g = 2 * j
                e0 = a_even[g * steps : (g + 1) * steps]
                o0 = a_odd[g * steps : (g + 1) * steps]
                e1 = a_even[(g + 1) * steps : (g + 2) * steps]
                o1 = a_odd[(g + 1) * steps : (g + 2) * steps]
                tile = jnp.where(
                    low_lanes, e0 + pltpu.roll(o0, HEAD_DIM, 1), o1 + pltpu.roll(e1, HEAD_DIM, 1)
                )
                att_ref[j, pl.ds(b, steps, stride=seqs), :] = tile
        return carry

    for copy in ready_copies + [key_copy, value_copy]:
        copy.wait()
    lax.fori_loop(0, seqs // TOGETHER, several, 0)

    out_weight_copy.wait()
    attended = jnp.concatenate([att_ref[j] for j in range(tiles)], axis=1).astype(jnp.bfloat16)
    low = lax.dot_general(
        attended, left_rows(left_o_ref[...]), CONTRACT_LAST, preferred_element_type=jnp.float32
    )
    low = low_rank_operand(low)
    for at in range(0, width, 768):
        to = min(at + 768, width)
        share = lax.dot_general(
            attended, out_weight_ref[at:to, :], CONTRACT_LAST, preferred_element_type=jnp.float32
        ) + jnp.dot(low, right_ref[:, at:to], preferred_element_type=jnp.float32)
        share = share.astype(jnp.bfloat16)
        part = total_rows // len(outs)
        for c, out in enumerate(outs):
            out[:, at:to] = share[c * part : (c + 1) * part]


def layer(
    lengths, sinks, place, chunks, ready, out_parts, weight, out_weight, keys, values, own_steps, *operands
):
    chunk_rows, width = chunks[0].shape
    rows = sum(r.shape[1] for r in ready) + chunk_rows * len(chunks)
    joined = weight.shape[1]
    qdim = operands[1].shape[1]
    group_rows = rows // values.shape[0] * qdim // HEAD_DIM
    vmem = pl.BlockSpec(memory_space=pltpu.VMEM)
    smem = pl.BlockSpec(memory_space=pltpu.SMEM)
    either = pl.BlockSpec(memory_space=pl.ANY)

    def kernel(*refs):
        layer_kernel(
            *refs, chunk_count=len(chunks), ready_count=len(ready), own_steps=own_steps
        )

    return pl.pallas_call(
        kernel,
        in_specs=[smem] * 3 + [either] * (len(chunks) + len(ready) + 4) + [vmem] * len(operands),
        out_specs=[vmem] * out_parts,
        out_shape=[jax.ShapeDtypeStruct((rows // out_parts, width), jnp.bfloat16)] * out_parts,
        scratch_shapes=[
            pltpu.VMEM((chunk_rows * len(chunks), width), jnp.bfloat16),
            pltpu.VMEM(weight.shape, jnp.bfloat16),
            pltpu.VMEM(out_weight.shape, jnp.bfloat16),
            pltpu.VMEM(keys.shape, jnp.bfloat16),
            pltpu.VMEM(values.shape, jnp.bfloat16),
            pltpu.VMEM((joined // LANES, rows, LANES), jnp.float32),
            pltpu.VMEM((qdim // LANES, rows, LANES), jnp.float32),
            pltpu.VMEM((LANES, width), jnp.bfloat16),
            pltpu.VMEM((group_rows, LANES), jnp.float32),
            pltpu.SemaphoreType.DMA((4,)),
            pltpu.SemaphoreType.DMA((len(chunks) + len(ready),)),
        ],
        compiler_params=pltpu.CompilerParams(vmem_limit_bytes=57 * 1024 * 1024),
    )(lengths, sinks, place, *chunks, *ready, weight, out_weight, keys, values, *operands)


def shards(
    hidden,
    joined_weight,
    output_weight,
    key_cache,
    value_cache,
    sink_logits,
    lengths,
    query_left,
    query_right,
    output_left,
    output_right,
    fitness,
    query_master,
    query_moment,
    output_master,
    output_moment,
):
    ring = lax.axis_size("head")
    place = lax.axis_index("head")
    right_pairs = [(i, (i + 1) % ring) for i in range(ring)]
    left_pairs = [(i, (i - 1) % ring) for i in range(ring)]

    def to_right(x):
        return lax.ppermute(x, "head", right_pairs)

    def to_left(x):
        return lax.ppermute(x, "head", left_pairs)

    _, own_steps, row_count, width = hidden.shape
    flat_weight = joined_weight[:, 0, :]

    member_count = lax.axis_size("member")
    factors = pack(fitness, query_left[0], output_right[0], query_right[0], output_left[0])
    held = [factors, factors]

    def exchange(distance, after):
        if distance < 1:
            return after
        mine = held[0]
        if held[1] is not held[0]:
            mine = jnp.concatenate(held, axis=0)
        mine, after = lax.optimization_barrier((mine, after))
        pairs = [(i, i ^ distance) for i in range(member_count)]
        held[0], held[1] = mine, lax.ppermute(mine, "member", pairs)
        return after

    keys, values = relayout(key_cache[0, 0], value_cache[0, 0])

    offsets = [0]
    for distance in range(1, ring // 2):
        offsets += [distance, -distance]
    offsets.append(ring // 2)
    chunk_ids = jnp.mod(place + jnp.array(offsets, jnp.int32), ring)
    steps = (
        chunk_ids[:, None] * own_steps + jnp.arange(own_steps, dtype=jnp.int32)[None, :]
    ).reshape(-1)
    half_dim = HEAD_DIM // 2
    lane_ids = jnp.arange(LANES, dtype=jnp.int32)
    exponents = (lane_ids % half_dim).astype(jnp.float32) * (-2.0 / HEAD_DIM)
    frequency = jnp.power(jnp.float32(rotary_base), exponents)
    positions = steps[:, None] + lengths[0][None, :]
    angles = positions.astype(jnp.float32)[..., None] * frequency
    sign = jnp.where(lane_ids % HEAD_DIM < half_dim, -1.0, 1.0).astype(jnp.float32)
    cosines = jnp.cos(angles).reshape(-1, LANES)
    sines = (jnp.sin(angles) * sign).reshape(-1, LANES)

    own = hidden[0].reshape(-1, width)
    half = own.shape[0] // 2
    exchange(member_count // 2, ())
    from_left, from_right = [own, to_right(own)], [own, to_left(own)]
    keys, values, cosines, sines, onward, back = lax.optimization_barrier(
        (keys, values, cosines, sines, from_left[1], from_right[1])
    )
    from_left.append(to_right(onward))
    from_right.append(to_left(back))
    exchange(member_count // 4, from_left[1])
    own_rows = own.shape[0]
    factor_operands = (flat_weight, query_left[0], query_right[0], cosines, sines)
    for distance in range(3, ring // 2):
        from_left.append(to_right(from_left[-1]))
        from_right.append(to_left(from_right[-1]))
    near = [own]
    for distance in range(1, ring // 2):
        near += [from_right[distance], from_left[distance]]
    early = ring - 3
    exchange(member_count // 8, from_left[-2])
    first_projected = project_chunks(near[:early], 0, *factor_operands)
    first_projected, onward, back = lax.optimization_barrier(
        (first_projected, from_left[-1][:half], from_right[-1][half:])
    )
    far = [to_right(onward), to_left(back)]
    second_projected = project_chunks(near[early:], early * own_rows, *factor_operands)
    exchange(member_count // 16, from_left[-1])
    projected = [first_projected, second_projected]
    shares = layer(
        lengths[0],
        sink_logits,
        place.reshape(1).astype(jnp.int32),
        far,
        projected,
        2 * ring,
        flat_weight,
        output_weight.T,
        keys,
        values,
        own_steps,
        query_left[0],
        query_right[0],
        output_left[0],
        output_right[0],
        cosines,
        sines,
    )

    exchange(member_count // 32, shares[0])
    row_share = query_master.shape[0]
    start = query_right.shape[2] + lax.axis_index("member") * row_share
    updated = update(
        start.reshape(1).astype(jnp.int32),
        *held,
        query_right.shape[1],
        member_count,
        query_moment,
        query_master,
        output_moment,
        output_master,
    )

    results = []
    for k in range(2):
        at = {offset: shares[2 * i + k] for i, offset in enumerate(offsets)}

        def plus(received, offset):
            return (received.astype(jnp.float32) + at[offset].astype(jnp.float32)).astype(
                jnp.bfloat16
            )

        last = ring // 2 - 1
        if k == 0:
            rightward = plus(to_right(at[last + 1]), last)
            leftward = at[-last]
        else:
            rightward = at[last]
            leftward = plus(to_left(at[last + 1]), -last)
        for distance in range(last - 1, 0, -1):
            rightward = plus(to_right(rightward), distance)
            leftward = plus(to_left(leftward), -distance)
        results.append((to_right(rightward), to_left(leftward), at[0]))
    mine, updated = lax.optimization_barrier(([r[2] for r in results], tuple(updated)))
    layer_output = []
    for (from_left, from_right, _), own_share in zip(results, mine):
        total = (
            from_left.astype(jnp.float32)
            + from_right.astype(jnp.float32)
            + own_share.astype(jnp.float32)
        )
        layer_output.append(total.astype(jnp.bfloat16).reshape(own_steps // 2, row_count, width))
    layer_output = jnp.concatenate(layer_output, axis=0)[None]
    return (layer_output,) + updated


def solution(mesh):
    placed = (
        P("member", "head", None, None),
        P(None, "head", None),
        P("head", None),
        P("member", "head", None, None),
        P("member", "head", None, None),
        P("head"),
        P("member", None),
        P("member", None, None),
        P("member", None, "head"),
        P("member", None, "head"),
        P("member", None, None),
        P("member"),
        P("member", "head"),
        P("member", "head"),
        P("member", "head"),
        P("member", "head"),
    )
    return jax.shard_map(
        shards,
        mesh=mesh,
        in_specs=placed,
        out_specs=(
            P("member", "head", None, None),
            P("member", "head"),
            P("member", "head"),
            P("member", "head"),
            P("member", "head"),
        ),
        check_vma=False,
    )
```

profile of v0, /device:TPU:8, one launch (start us, length us, event | category | flops | bytes accessed | tf_op | source)
XLA Modules:
  0.0 112.5 jit_solution(2901958519138182997)
XLA Ops:
  0.6 2.0 %collective-permute-start.1 = (bf16[64,2880]{1,0:T(8,128)(2,1)}, bf16[64,2880]{1,0:T(8,128)(2,1)S(1)}, u32[]{:S(2)}, u32[]{:S(2)}) collective-permute-start(bf16[64,2880]{1,0:T(8,128)(2,1)} %bitcast.30), channel_id=1, source_target_pairs={{0,1},{1,2},{2,3},{3,4},{4,5},{5,6},{6,7},{7,0},{8,9},{9,10},{10,1... | collective-permute-start | bytes 1105928 | tf_op jit(solution)/shard_map/ppermute | solution.py:546
  2.6 4.0 %collective-permute-start = (bf16[64,2880]{1,0:T(8,128)(2,1)}, bf16[64,2880]{1,0:T(8,128)(2,1)S(1)}, u32[]{:S(2)}, u32[]{:S(2)}) collective-permute-start(bf16[64,2880]{1,0:T(8,128)(2,1)} %bitcast.31), channel_id=1, source_target_pairs={{0,7},{1,0},{2,1},{3,2},{4,3},{5,4},{6,5},{7,6},{8,15},{9,8},{10,9... | collective-permute-start | bytes 1105928 | tf_op jit(solution)/shard_map/ppermute | solution.py:549
  7.3 1.5 %shard_map.204 = bf16[8,3456]{1,0:T(8,128)(2,1)} custom-call(f32[1]{0:T(128)S(6)} %copy.22.fitness_ref, f32[4,2880]{1,0:T(4,128)} %bitcast.26, f32[4,2880]{1,0:T(4,128)} %bitcast.33, f32[4,512]{1,0:T(4,128)} %bitcast.35, f32[4,512]{1,0:T(4,128)} %bitcast.39), custom_call_target="tpu_custom_call" | custom-call | tf_op jit(solution)/shard_map/pallas_call | solution.py:97
  8.8 2.3 %collective-permute-start.15 = (bf16[8,3456]{1,0:T(8,128)(2,1)}, bf16[8,3456]{1,0:T(8,128)(2,1)S(1)}, u32[]{:S(2)}, u32[]{:S(2)}) collective-permute-start(bf16[8,3456]{1,0:T(8,128)(2,1)} %shard_map.204), channel_id=1, source_target_pairs={{0,128},{8,136},{16,144},{24,152},{32,160},{40,168},{48,176},{56,1... | collective-permute-start | bytes 165896 | tf_op jit(solution)/shard_map/ppermute | solution.py:566
  12.8 1.8 %fusion = (f32[512,128]{1,0:T(8,128)}, f32[512,128]{1,0:T(8,128)}) fusion(f32[128]{0:T(128)S(1)} %get-tuple-element.89, f32[128]{0:T(128)S(1)} %get-tuple-element.90, f32[512]{0:T(512)S(1)} %add_convert_fusion.12), kind=kLoop, calls=%fused_computation.17 | loop fusion | flops 131072 | bytes 527360 | tf_op jit(solution)/shard_map/mul | solution.py:587
  14.6 5.0 %shard_map.200 = (bf16[16,512,128]{2,1,0:T(8,128)(2,1)}, bf16[16,512,128]{2,1,0:T(8,128)(2,1)}) custom-call(bf16[16,65536]{1,0:T(8,128)(2,1)} %bitcast.22, bf16[16,65536]{1,0:T(8,128)(2,1)} %bitcast.23), custom_call_target="tpu_custom_call" | custom-call | tf_op jit(solution)/shard_map/pallas_call | solution.py:67
  19.7 2.0 %collective-permute-start.2 = (bf16[64,2880]{1,0:T(8,128)(2,1)S(1)}, bf16[64,2880]{1,0:T(8,128)(2,1)S(1)}, u32[]{:S(2)}, u32[]{:S(2)}) collective-permute-start(bf16[64,2880]{1,0:T(8,128)(2,1)S(1)} %collective-permute-done.refs_1_), channel_id=1, source_target_pairs={{0,7},{1,0},{2,1},{3,2},{4,3},{5,4},{6,5},{7,6},{8,15},{9,8},{10,9... | collective-permute-start | bytes 1105928 | tf_op jit(solution)/shard_map/ppermute | solution.py:549
  23.2 6.5 %collective-permute-done.2.refs_3_ = bf16[64,2880]{1,0:T(8,128)(2,1)S(1)} collective-permute-done((bf16[64,2880]{1,0:T(8,128)(2,1)S(1)}, bf16[64,2880]{1,0:T(8,128)(2,1)S(1)}, u32[]{:S(2)}, u32[]{:S(2)}) %collective-permute-start.2) | collective-permute-done | bytes 368672 | tf_op jit(solution)/shard_map/ppermute | solution.py:549
  29.7 2.9 %collective-permute-start.5 = (bf16[64,2880]{1,0:T(8,128)(2,1)S(1)}, bf16[64,2880]{1,0:T(8,128)(2,1)S(1)}, u32[]{:S(2)}, u32[]{:S(2)}) collective-permute-start(bf16[64,2880]{1,0:T(8,128)(2,1)S(1)} %collective-permute-done.2.refs_3_), channel_id=1, source_target_pairs={{0,7},{1,0},{2,1},{3,2},{4,3},{5,4},{6,5},{7,6},{8,15},{9,8},{10,9... | collective-permute-start | bytes 1105928 | tf_op jit(solution)/shard_map/ppermute | solution.py:549
  32.6 3.3 %collective-permute-start.17 = (bf16[32,3456]{1,0:T(8,128)(2,1)S(1)}, bf16[32,3456]{1,0:T(8,128)(2,1)S(1)}, u32[]{:S(2)}, u32[]{:S(2)}) collective-permute-start(bf16[32,3456]{1,0:T(8,128)(2,1)S(1)} %pad_maximum_fusion.2), channel_id=1, source_target_pairs={{0,32},{8,40},{16,48},{24,56},{32,0},{40,8},{48,16},{56,24},{64,96... | collective-permute-start | bytes 663560 | tf_op jit(solution)/shard_map/ppermute | solution.py:566
  35.9 7.2 %shard_map.201.refs_5_ = f32[5,320,128]{2,1,0:T(8,128)} custom-call(bf16[64,2880]{1,0:T(8,128)(2,1)} %bitcast.32, bf16[64,2880]{1,0:T(8,128)(2,1)} %copy-done.7, bf16[64,2880]{1,0:T(8,128)(2,1)} %copy-done.6, bf16[64,2880]{1,0:T(8,128)(2,1)} %copy-done.9, bf16[64,2880]{1,0:T(8,128)(2,1)} %copy-done.8, bf16[2880,640]{1,0:T(8,128)(2,1)} %bitcast.18, ...), custom_call_target="tpu_custom_call" | custom-call | tf_op jit(solution)/shard_map/pallas_call | solution.py:269
  43.3 3.3 %collective-permute-start.7 = (bf16[32,2880]{1,0:T(8,128)(2,1)S(1)}, bf16[32,2880]{1,0:T(8,128)(2,1)S(1)}, u32[]{:S(2)}, u32[]{:S(2)}) collective-permute-start(bf16[32,2880]{1,0:T(8,128)(2,1)S(1)} %slice.9), channel_id=1, source_target_pairs={{0,7},{1,0},{2,1},{3,2},{4,3},{5,4},{6,5},{7,6},{8,15},{9,8},{10,9... | collective-permute-start | bytes 552968 | tf_op jit(solution)/shard_map/ppermute | solution.py:549
  46.6 5.2 %shard_map.202.refs_6_ = f32[5,128,128]{2,1,0:T(8,128)} custom-call(bf16[64,2880]{1,0:T(8,128)(2,1)} %copy-done.4, bf16[64,2880]{1,0:T(8,128)(2,1)} %copy-done.5, bf16[2880,640]{1,0:T(8,128)(2,1)} %bitcast.19, f32[4,2880]{1,0:T(4,128)} %bitcast.28, f32[4,512]{1,0:T(4,128)} %bitcast.37, f32[512,128]{1,0:T(8,128)} %get-tuple-element.50.refs_8_.refs_5_.refs_15_, ...), custom_call_target="tpu_custom_call" | custom-call | tf_op jit(solution)/shard_map/pallas_call | solution.py:269
  52.5 18.6 %shard_map.203 = (bf16[32,2880]{1,0:T(8,128)(2,1)}, bf16[32,2880]{1,0:T(8,128)(2,1)}, bf16[32,2880]{1,0:T(8,128)(2,1)}, bf16[32,2880]{1,0:T(8,128)(2,1)}, bf16[3...) custom-call(s32[16]{0:T(128)} %bitcast.42, ...), custom_call_target="tpu_custom_call" | custom-call | tf_op jit(solution)/shard_map/pallas_call | solution.py:500
  72.0 3.2 %collective-permute-start.12 = (bf16[32,2880]{1,0:T(8,128)(2,1)}, bf16[32,2880]{1,0:T(8,128)(2,1)S(1)}, u32[]{:S(2)}, u32[]{:S(2)}) collective-permute-start(bf16[32,2880]{1,0:T(8,128)(2,1)} %get-tuple-element.61), channel_id=1, source_target_pairs={{0,7},{1,0},{2,1},{3,2},{4,3},{5,4},{6,5},{7,6},{8,15},{9,8},{10,9... | collective-permute-start | bytes 552968 | tf_op jit(solution)/shard_map/ppermute | solution.py:549
  75.2 3.2 %collective-permute-start.23 = (bf16[32,2880]{1,0:T(8,128)(2,1)}, bf16[32,2880]{1,0:T(8,128)(2,1)S(1)}, u32[]{:S(2)}, u32[]{:S(2)}) collective-permute-start(bf16[32,2880]{1,0:T(8,128)(2,1)} %get-tuple-element.78), channel_id=1, source_target_pairs={{0,7},{1,0},{2,1},{3,2},{4,3},{5,4},{6,5},{7,6},{8,15},{9,8},{10,9... | collective-permute-start | bytes 552968 | tf_op jit(solution)/shard_map/ppermute | solution.py:549
  81.8 3.3 %collective-permute-start.13 = (bf16[32,2880]{1,0:T(8,128)(2,1)S(1)}, bf16[32,2880]{1,0:T(8,128)(2,1)S(1)}, u32[]{:S(2)}, u32[]{:S(2)}) collective-permute-start(bf16[32,2880]{1,0:T(8,128)(2,1)S(1)} %add_convert_fusion.8), channel_id=1, source_target_pairs={{0,7},{1,0},{2,1},{3,2},{4,3},{5,4},{6,5},{7,6},{8,15},{9,8},{10,9... | collective-permute-start | bytes 552968 | tf_op jit(solution)/shard_map/ppermute | solution.py:549
  85.4 3.3 %collective-permute-start.24 = (bf16[32,2880]{1,0:T(8,128)(2,1)S(1)}, bf16[32,2880]{1,0:T(8,128)(2,1)S(1)}, u32[]{:S(2)}, u32[]{:S(2)}) collective-permute-start(bf16[32,2880]{1,0:T(8,128)(2,1)S(1)} %add_convert_fusion.3), channel_id=1, source_target_pairs={{0,7},{1,0},{2,1},{3,2},{4,3},{5,4},{6,5},{7,6},{8,15},{9,8},{10,9... | collective-permute-start | bytes 552968 | tf_op jit(solution)/shard_map/ppermute | solution.py:549
  89.1 3.3 %collective-permute-start.14 = (bf16[32,2880]{1,0:T(8,128)(2,1)S(1)}, bf16[32,2880]{1,0:T(8,128)(2,1)S(1)}, u32[]{:S(2)}, u32[]{:S(2)}) collective-permute-start(bf16[32,2880]{1,0:T(8,128)(2,1)S(1)} %add_convert_fusion.7), channel_id=1, source_target_pairs={{0,7},{1,0},{2,1},{3,2},{4,3},{5,4},{6,5},{7,6},{8,15},{9,8},{10,9... | collective-permute-start | bytes 552968 | tf_op jit(solution)/shard_map/ppermute | solution.py:549
  92.5 3.1 %collective-permute-start.25 = (bf16[32,2880]{1,0:T(8,128)(2,1)S(1)}, bf16[32,2880]{1,0:T(8,128)(2,1)S(1)}, u32[]{:S(2)}, u32[]{:S(2)}) collective-permute-start(bf16[32,2880]{1,0:T(8,128)(2,1)S(1)} %add_convert_fusion.2), channel_id=1, source_target_pairs={{0,7},{1,0},{2,1},{3,2},{4,3},{5,4},{6,5},{7,6},{8,15},{9,8},{10,9... | collective-permute-start | bytes 552968 | tf_op jit(solution)/shard_map/ppermute | solution.py:549
  95.7 5.1 %collective-permute-done.25 = bf16[32,2880]{1,0:T(8,128)(2,1)S(1)} collective-permute-done((bf16[32,2880]{1,0:T(8,128)(2,1)S(1)}, bf16[32,2880]{1,0:T(8,128)(2,1)S(1)}, u32[]{:S(2)}, u32[]{:S(2)}) %collective-permute-start.25) | collective-permute-done | bytes 184352 | tf_op jit(solution)/shard_map/ppermute | solution.py:549
  100.9 3.8 %collective-permute-start.26 = (bf16[32,2880]{1,0:T(8,128)(2,1)S(1)}, bf16[32,2880]{1,0:T(8,128)(2,1)S(1)}, u32[]{:S(2)}, u32[]{:S(2)}) collective-permute-start(bf16[32,2880]{1,0:T(8,128)(2,1)S(1)} %add_convert_fusion.1), channel_id=1, source_target_pairs={{0,7},{1,0},{2,1},{3,2},{4,3},{5,4},{6,5},{7,6},{8,15},{9,8},{10,9... | collective-permute-start | bytes 552968 | tf_op jit(solution)/shard_map/ppermute | solution.py:549
  106.1 2.0 %collective-permute-done.26 = bf16[32,2880]{1,0:T(8,128)(2,1)S(1)} collective-permute-done((bf16[32,2880]{1,0:T(8,128)(2,1)S(1)}, bf16[32,2880]{1,0:T(8,128)(2,1)S(1)}, u32[]{:S(2)}, u32[]{:S(2)}) %collective-permute-start.26) | collective-permute-done | bytes 184352 | tf_op jit(solution)/shard_map/ppermute | solution.py:549
  108.2 3.5 %collective-permute-done.11 = bf16[32,2880]{1,0:T(8,128)(2,1)S(1)} collective-permute-done((bf16[32,2880]{1,0:T(8,128)(2,1)S(1)}, bf16[32,2880]{1,0:T(8,128)(2,1)S(1)}, u32[]{:S(2)}, u32[]{:S(2)}) %collective-permute-start.11) | collective-permute-done | bytes 184352 | tf_op jit(solution)/shard_map/ppermute | solution.py:546
  (111 shorter events, 11.5 us)
Async XLA Ops:
  0.6 19.0 %collective-permute-start.1 = (bf16[64,2880]{1,0:T(8,128)(2,1)}, bf16[64,2880]{1,0:T(8,128)(2,1)S(1)}, u32[]{:S(2)}, u32[]{:S(2)}) collective-permute-start(bf16[64,2880]{1,0:T(8,128)(2,1)} %bitcast.30), channel_id=1, source_target_pairs={{0,1},{1,2},{2,3},{3,4},{4,5},{5,6},{6,7},{7,0},{8,9},{9,10},{10,1... | collective-permute-start | bytes 1105928 | tf_op jit(solution)/shard_map/ppermute | solution.py:546
  2.6 17.0 %collective-permute-start = (bf16[64,2880]{1,0:T(8,128)(2,1)}, bf16[64,2880]{1,0:T(8,128)(2,1)S(1)}, u32[]{:S(2)}, u32[]{:S(2)}) collective-permute-start(bf16[64,2880]{1,0:T(8,128)(2,1)} %bitcast.31), channel_id=1, source_target_pairs={{0,7},{1,0},{2,1},{3,2},{4,3},{5,4},{6,5},{7,6},{8,15},{9,8},{10,9... | collective-permute-start | bytes 1105928 | tf_op jit(solution)/shard_map/ppermute | solution.py:549
  8.8 13.0 %collective-permute-start.15 = (bf16[8,3456]{1,0:T(8,128)(2,1)}, bf16[8,3456]{1,0:T(8,128)(2,1)S(1)}, u32[]{:S(2)}, u32[]{:S(2)}) collective-permute-start(bf16[8,3456]{1,0:T(8,128)(2,1)} %shard_map.204), channel_id=1, source_target_pairs={{0,128},{8,136},{16,144},{24,152},{32,160},{40,168},{48,176},{56,1... | collective-permute-start | bytes 165896 | tf_op jit(solution)/shard_map/ppermute | solution.py:566
  19.7 10.0 %collective-permute-start.2 = (bf16[64,2880]{1,0:T(8,128)(2,1)S(1)}, bf16[64,2880]{1,0:T(8,128)(2,1)S(1)}, u32[]{:S(2)}, u32[]{:S(2)}) collective-permute-start(bf16[64,2880]{1,0:T(8,128)(2,1)S(1)} %collective-permute-done.refs_1_), channel_id=1, source_target_pairs={{0,7},{1,0},{2,1},{3,2},{4,3},{5,4},{6,5},{7,6},{8,15},{9,8},{10,9... | collective-permute-start | bytes 1105928 | tf_op jit(solution)/shard_map/ppermute | solution.py:549
  21.7 10.9 %collective-permute-start.3 = (bf16[64,2880]{1,0:T(8,128)(2,1)S(1)}, bf16[64,2880]{1,0:T(8,128)(2,1)S(1)}, u32[]{:S(2)}, u32[]{:S(2)}) collective-permute-start(bf16[64,2880]{1,0:T(8,128)(2,1)S(1)} %collective-permute-done.1.refs_2_), channel_id=1, source_target_pairs={{0,1},{1,2},{2,3},{3,4},{4,5},{5,6},{6,7},{7,0},{8,9},{9,10},{10,1... | collective-permute-start | bytes 1105928 | tf_op jit(solution)/shard_map/ppermute | solution.py:546
  21.8 10.8 %collective-permute-start.16 = (bf16[16,3456]{1,0:T(8,128)(2,1)S(1)}, bf16[16,3456]{1,0:T(8,128)(2,1)S(1)}, u32[]{:S(2)}, u32[]{:S(2)}) collective-permute-start(bf16[16,3456]{1,0:T(8,128)(2,1)S(1)} %pad_maximum_fusion.3), channel_id=1, source_target_pairs={{0,64},{8,72},{16,80},{24,88},{32,96},{40,104},{48,112},{56,120},{... | collective-permute-start | bytes 331784 | tf_op jit(solution)/shard_map/ppermute | solution.py:566
  29.7 13.4 %collective-permute-start.5 = (bf16[64,2880]{1,0:T(8,128)(2,1)S(1)}, bf16[64,2880]{1,0:T(8,128)(2,1)S(1)}, u32[]{:S(2)}, u32[]{:S(2)}) collective-permute-start(bf16[64,2880]{1,0:T(8,128)(2,1)S(1)} %collective-permute-done.2.refs_3_), channel_id=1, source_target_pairs={{0,7},{1,0},{2,1},{3,2},{4,3},{5,4},{6,5},{7,6},{8,15},{9,8},{10,9... | collective-permute-start | bytes 1105928 | tf_op jit(solution)/shard_map/ppermute | solution.py:549
  32.6 10.6 %collective-permute-start.4 = (bf16[64,2880]{1,0:T(8,128)(2,1)S(1)}, bf16[64,2880]{1,0:T(8,128)(2,1)S(1)}, u32[]{:S(2)}, u32[]{:S(2)}) collective-permute-start(bf16[64,2880]{1,0:T(8,128)(2,1)S(1)} %collective-permute-done.3.refs_4_), channel_id=1, source_target_pairs={{0,1},{1,2},{2,3},{3,4},{4,5},{5,6},{6,7},{7,0},{8,9},{9,10},{10,1... | collective-permute-start | bytes 1105928 | tf_op jit(solution)/shard_map/ppermute | solution.py:546
  32.6 38.7 %collective-permute-start.17 = (bf16[32,3456]{1,0:T(8,128)(2,1)S(1)}, bf16[32,3456]{1,0:T(8,128)(2,1)S(1)}, u32[]{:S(2)}, u32[]{:S(2)}) collective-permute-start(bf16[32,3456]{1,0:T(8,128)(2,1)S(1)} %pad_maximum_fusion.2), channel_id=1, source_target_pairs={{0,32},{8,40},{16,48},{24,56},{32,0},{40,8},{48,16},{56,24},{64,96... | collective-permute-start | bytes 663560 | tf_op jit(solution)/shard_map/ppermute | solution.py:566
  43.2 8.6 %collective-permute-start.6 = (bf16[32,2880]{1,0:T(8,128)(2,1)S(1)}, bf16[32,2880]{1,0:T(8,128)(2,1)S(1)}, u32[]{:S(2)}, u32[]{:S(2)}) collective-permute-start(bf16[32,2880]{1,0:T(8,128)(2,1)S(1)} %slice.8), channel_id=1, source_target_pairs={{0,1},{1,2},{2,3},{3,4},{4,5},{5,6},{6,7},{7,0},{8,9},{9,10},{10,1... | collective-permute-start | bytes 552968 | tf_op jit(solution)/shard_map/ppermute | solution.py:546
  43.3 8.5 %collective-permute-start.7 = (bf16[32,2880]{1,0:T(8,128)(2,1)S(1)}, bf16[32,2880]{1,0:T(8,128)(2,1)S(1)}, u32[]{:S(2)}, u32[]{:S(2)}) collective-permute-start(bf16[32,2880]{1,0:T(8,128)(2,1)S(1)} %slice.9), channel_id=1, source_target_pairs={{0,7},{1,0},{2,1},{3,2},{4,3},{5,4},{6,5},{7,6},{8,15},{9,8},{10,9... | collective-permute-start | bytes 552968 | tf_op jit(solution)/shard_map/ppermute | solution.py:549
  71.2 8.6 %collective-permute-start.8 = (bf16[32,2880]{1,0:T(8,128)(2,1)}, bf16[32,2880]{1,0:T(8,128)(2,1)S(1)}, u32[]{:S(2)}, u32[]{:S(2)}) collective-permute-start(bf16[32,2880]{1,0:T(8,128)(2,1)} %get-tuple-element.57), channel_id=1, source_target_pairs={{0,1},{1,2},{2,3},{3,4},{4,5},{5,6},{6,7},{7,0},{8,9},{9,10},{10,1... | collective-permute-start | bytes 552968 | tf_op jit(solution)/shard_map/ppermute | solution.py:546
  71.3 17.3 %collective-permute-start.18 = (bf16[64,3456]{1,0:T(8,128)(2,1)S(1)}, bf16[64,3456]{1,0:T(8,128)(2,1)S(1)}, u32[]{:S(2)}, u32[]{:S(2)}) collective-permute-start(bf16[64,3456]{1,0:T(8,128)(2,1)S(1)} %pad_maximum_fusion.1), channel_id=1, source_target_pairs={{0,16},{8,24},{16,0},{24,8},{32,48},{40,56},{48,32},{56,40},{64,80... | collective-permute-start | bytes 1327112 | tf_op jit(solution)/shard_map/ppermute | solution.py:566
  72.0 8.8 %collective-permute-start.12 = (bf16[32,2880]{1,0:T(8,128)(2,1)}, bf16[32,2880]{1,0:T(8,128)(2,1)S(1)}, u32[]{:S(2)}, u32[]{:S(2)}) collective-permute-start(bf16[32,2880]{1,0:T(8,128)(2,1)} %get-tuple-element.61), channel_id=1, source_target_pairs={{0,7},{1,0},{2,1},{3,2},{4,3},{5,4},{6,5},{7,6},{8,15},{9,8},{10,9... | collective-permute-start | bytes 552968 | tf_op jit(solution)/shard_map/ppermute | solution.py:549
  75.2 9.9 %collective-permute-start.20 = (bf16[32,2880]{1,0:T(8,128)(2,1)}, bf16[32,2880]{1,0:T(8,128)(2,1)S(1)}, u32[]{:S(2)}, u32[]{:S(2)}) collective-permute-start(bf16[32,2880]{1,0:T(8,128)(2,1)} %get-tuple-element.75), channel_id=1, source_target_pairs={{0,1},{1,2},{2,3},{3,4},{4,5},{5,6},{6,7},{7,0},{8,9},{9,10},{10,1... | collective-permute-start | bytes 552968 | tf_op jit(solution)/shard_map/ppermute | solution.py:546
  75.2 10.1 %collective-permute-start.23 = (bf16[32,2880]{1,0:T(8,128)(2,1)}, bf16[32,2880]{1,0:T(8,128)(2,1)S(1)}, u32[]{:S(2)}, u32[]{:S(2)}) collective-permute-start(bf16[32,2880]{1,0:T(8,128)(2,1)} %get-tuple-element.78), channel_id=1, source_target_pairs={{0,7},{1,0},{2,1},{3,2},{4,3},{5,4},{6,5},{7,6},{8,15},{9,8},{10,9... | collective-permute-start | bytes 552968 | tf_op jit(solution)/shard_map/ppermute | solution.py:549
  80.7 8.1 %collective-permute-start.9 = (bf16[32,2880]{1,0:T(8,128)(2,1)S(1)}, bf16[32,2880]{1,0:T(8,128)(2,1)S(1)}, u32[]{:S(2)}, u32[]{:S(2)}) collective-permute-start(bf16[32,2880]{1,0:T(8,128)(2,1)S(1)} %add_convert_fusion.11), channel_id=1, source_target_pairs={{0,1},{1,2},{2,3},{3,4},{4,5},{5,6},{6,7},{7,0},{8,9},{9,10},{10,1... | collective-permute-start | bytes 552968 | tf_op jit(solution)/shard_map/ppermute | solution.py:546
  85.2 10.4 %collective-permute-start.21 = (bf16[32,2880]{1,0:T(8,128)(2,1)S(1)}, bf16[32,2880]{1,0:T(8,128)(2,1)S(1)}, u32[]{:S(2)}, u32[]{:S(2)}) collective-permute-start(bf16[32,2880]{1,0:T(8,128)(2,1)S(1)} %add_convert_fusion.5), channel_id=1, source_target_pairs={{0,1},{1,2},{2,3},{3,4},{4,5},{5,6},{6,7},{7,0},{8,9},{9,10},{10,1... | collective-permute-start | bytes 552968 | tf_op jit(solution)/shard_map/ppermute | solution.py:546
  88.8 16.0 %collective-permute-start.19 = (bf16[128,3456]{1,0:T(8,128)(2,1)S(1)}, bf16[128,3456]{1,0:T(8,128)(2,1)S(1)}, u32[]{:S(2)}, u32[]{:S(2)}) collective-permute-start(bf16[128,3456]{1,0:T(8,128)(2,1)S(1)} %pad_maximum_fusion.refs_1_), channel_id=1, source_target_pairs={{0,8},{8,0},{16,24},{24,16},{32,40},{40,32},{48,56},{56,48},{64,72... | collective-permute-start | bytes 2654216 | tf_op jit(solution)/shard_map/ppermute | solution.py:566
  89.0 15.7 %collective-permute-start.10 = (bf16[32,2880]{1,0:T(8,128)(2,1)S(1)}, bf16[32,2880]{1,0:T(8,128)(2,1)S(1)}, u32[]{:S(2)}, u32[]{:S(2)}) collective-permute-start(bf16[32,2880]{1,0:T(8,128)(2,1)S(1)} %add_convert_fusion.10), channel_id=1, source_target_pairs={{0,1},{1,2},{2,3},{3,4},{4,5},{5,6},{6,7},{7,0},{8,9},{9,10},{10,1... | collective-permute-start | bytes 552968 | tf_op jit(solution)/shard_map/ppermute | solution.py:546
  89.1 19.1 %collective-permute-start.14 = (bf16[32,2880]{1,0:T(8,128)(2,1)S(1)}, bf16[32,2880]{1,0:T(8,128)(2,1)S(1)}, u32[]{:S(2)}, u32[]{:S(2)}) collective-permute-start(bf16[32,2880]{1,0:T(8,128)(2,1)S(1)} %add_convert_fusion.7), channel_id=1, source_target_pairs={{0,7},{1,0},{2,1},{3,2},{4,3},{5,4},{6,5},{7,6},{8,15},{9,8},{10,9... | collective-permute-start | bytes 552968 | tf_op jit(solution)/shard_map/ppermute | solution.py:549
  92.5 8.3 %collective-permute-start.25 = (bf16[32,2880]{1,0:T(8,128)(2,1)S(1)}, bf16[32,2880]{1,0:T(8,128)(2,1)S(1)}, u32[]{:S(2)}, u32[]{:S(2)}) collective-permute-start(bf16[32,2880]{1,0:T(8,128)(2,1)S(1)} %add_convert_fusion.2), channel_id=1, source_target_pairs={{0,7},{1,0},{2,1},{3,2},{4,3},{5,4},{6,5},{7,6},{8,15},{9,8},{10,9... | collective-permute-start | bytes 552968 | tf_op jit(solution)/shard_map/ppermute | solution.py:549
  95.6 10.4 %collective-permute-start.22 = (bf16[32,2880]{1,0:T(8,128)(2,1)S(1)}, bf16[32,2880]{1,0:T(8,128)(2,1)S(1)}, u32[]{:S(2)}, u32[]{:S(2)}) collective-permute-start(bf16[32,2880]{1,0:T(8,128)(2,1)S(1)} %add_convert_fusion.4), channel_id=1, source_target_pairs={{0,1},{1,2},{2,3},{3,4},{4,5},{5,6},{6,7},{7,0},{8,9},{9,10},{10,1... | collective-permute-start | bytes 552968 | tf_op jit(solution)/shard_map/ppermute | solution.py:546
  100.9 7.3 %collective-permute-start.26 = (bf16[32,2880]{1,0:T(8,128)(2,1)S(1)}, bf16[32,2880]{1,0:T(8,128)(2,1)S(1)}, u32[]{:S(2)}, u32[]{:S(2)}) collective-permute-start(bf16[32,2880]{1,0:T(8,128)(2,1)S(1)} %add_convert_fusion.1), channel_id=1, source_target_pairs={{0,7},{1,0},{2,1},{3,2},{4,3},{5,4},{6,5},{7,6},{8,15},{9,8},{10,9... | collective-permute-start | bytes 552968 | tf_op jit(solution)/shard_map/ppermute | solution.py:549
  (26 other events, 276.1 us)
where the time goes:
time: 113 us
  starting transfers between devices  45.8 us (41%)
  Pallas kernels  38.7 us (34%)
  waiting for transfers between devices  18.4 us (16%)
  other arithmetic  5.98 us (5%)
  local copies, waits for them, and re-layouts  1.83 us (2%)
  between operations  1.81 us (2%)
    ppermute x11, starting transfers between devices, to_left(): return lax.ppermute(x, 'head', left_pairs)  35.4 us
    pallas_call x1, Pallas kernels, layer(): pl.pallas_call(kernel, in_specs=[smem] * 3 + [either] * (len(chunks) + le...  18.6 us
    ppermute x11, waiting for transfers between devices, to_left(): return lax.ppermute(x, 'head', left_pairs)  13.6 us
    pallas_call x2, Pallas kernels, project_chunks(): pl.pallas_call(kernel, in_specs=[either] * (len(chunks) + 1) + [vmem] * 4...  12.4 us
    ppermute x5, starting transfers between devices, exchange(): held[0], held[1] = (mine, lax.ppermute(mine, 'member', pairs))  7.78 us
    pallas_call x1, Pallas kernels, relayout(): pl.pallas_call(relayout_kernel, in_specs=[hbm] * 2, out_specs=[hbm] * 2,...  4.99 us
    ppermute x11, waiting for transfers between devices, to_right(): return lax.ppermute(x, 'head', right_pairs)  4.78 us
    ppermute x11, starting transfers between devices, to_right(): return lax.ppermute(x, 'head', right_pairs)  2.68 us
  transfers between devices with their start and end apart: 27, of which 5 were waited for; matrix products, arithmetic and copies ran while one was open for 5% of the time, Pallas kernels for 34%

commit v1 on v0

--- a/solution.py
+++ b/solution.py
@@ -192,7 +192,7 @@
 CONTRACT_LAST = (((1,), (1,)), ((), ()))
 
 
-def project(tokens, weight_wait, weight_ref, left_q, right_q, cosines, sines, store):
+def project(tokens, weight_ref, left_q, right_q, cosines, sines, store):
     qdim = right_q.shape[1]
     tiles = qdim // LANES
     low = lax.dot_general(
@@ -212,7 +212,6 @@
         )
         return t * cosines + swapped * sines
 
-    weight_wait()
     proj = jnp.dot(tokens, weight_ref[...], preferred_element_type=jnp.float32)
     for j in range(tiles):
         part = slice(j * LANES, (j + 1) * LANES)
@@ -223,10 +222,10 @@
 
 def project_kernel(*refs, chunk_count, first_row):
     chunks = refs[:chunk_count]
-    weight_hbm, left_q_ref, right_q_ref, cos_ref, sin_ref, out_ref = refs[
+    weight_ref, left_q_ref, right_q_ref, cos_ref, sin_ref, out_ref = refs[
         chunk_count : chunk_count + 6
     ]
-    token_ref, weight_ref, sems = refs[chunk_count + 6 :]
+    token_ref, sems = refs[chunk_count + 6 :]
     chunk_rows = chunks[0].shape[0]
     rows = chunk_rows * chunk_count
     copies = [
@@ -235,8 +234,7 @@
         )
         for c in range(chunk_count)
     ]
-    weight_copy = pltpu.make_async_copy(weight_hbm, weight_ref, sems.at[chunk_count])
-    for copy in copies + [weight_copy]:
+    for copy in copies:
         copy.start()
     for copy in copies:
         copy.wait()
@@ -247,7 +245,6 @@
 
     project(
         token_ref[...],
-        weight_copy.wait,
         weight_ref,
         left_q_ref[...],
         right_q_ref[...],
@@ -268,19 +265,18 @@
 
     return pl.pallas_call(
         kernel,
-        in_specs=[either] * (len(chunks) + 1) + [vmem] * 4,
+        in_specs=[either] * len(chunks) + [vmem] * 5,
         out_specs=vmem,
         out_shape=jax.ShapeDtypeStruct((weight.shape[1] // LANES, rows, LANES), jnp.float32),
         scratch_shapes=[
             pltpu.VMEM((rows, width), jnp.bfloat16),
-            pltpu.VMEM(weight.shape, jnp.bfloat16),
-            pltpu.SemaphoreType.DMA((len(chunks) + 1,)),
+            pltpu.SemaphoreType.DMA((len(chunks),)),
         ],
-        compiler_params=pltpu.CompilerParams(vmem_limit_bytes=57 * 1024 * 1024),
+        compiler_params=pltpu.CompilerParams(vmem_limit_bytes=38 * 1024 * 1024),
     )(*chunks, weight, left_q, right_q, cosines, sines)
 
 
-TOGETHER = 2
+TOGETHER = 4
 
 
 def layer_kernel(lengths_ref, sink_ref, place_ref, *refs, chunk_count, ready_count, own_steps):
@@ -288,10 +284,10 @@
     ready = refs[chunk_count : chunk_count + ready_count]
     refs = refs[chunk_count + ready_count :]
     (
-        weight_hbm,
         out_weight_hbm,
         key_hbm,
         value_hbm,
+        weight_ref,
         left_q_ref,
         right_q_ref,
         left_o_ref,
@@ -301,7 +297,6 @@
     ) = refs[:10]
     (
         token_ref,
-        weight_ref,
         out_weight_ref,
         key_ref,
         value_ref,
@@ -311,8 +306,8 @@
         bias_ref,
         sems,
         chunk_sems,
-    ) = refs[-11:]
-    outs = refs[10:-11]
+    ) = refs[-10:]
+    outs = refs[10:-10]
     chunk_rows, width = chunks[0].shape
     copies = [
         pltpu.make_async_copy(
@@ -320,10 +315,9 @@
         )
         for c in range(chunk_count)
     ]
-    weight_copy = pltpu.make_async_copy(weight_hbm, weight_ref, sems.at[0])
-    key_copy = pltpu.make_async_copy(key_hbm, key_ref, sems.at[1])
-    value_copy = pltpu.make_async_copy(value_hbm, value_ref, sems.at[2])
-    out_weight_copy = pltpu.make_async_copy(out_weight_hbm, out_weight_ref, sems.at[3])
+    key_copy = pltpu.make_async_copy(key_hbm, key_ref, sems.at[0])
+    value_copy = pltpu.make_async_copy(value_hbm, value_ref, sems.at[1])
+    out_weight_copy = pltpu.make_async_copy(out_weight_hbm, out_weight_ref, sems.at[2])
     ready_copies = []
     first_row = 0
     for i in range(ready_count):
@@ -334,7 +328,7 @@
             )
         )
         first_row += count
-    for copy in copies + [weight_copy] + ready_copies + [key_copy, value_copy, out_weight_copy]:
+    for copy in copies + ready_copies + [key_copy, value_copy, out_weight_copy]:
         copy.start()
 
     seqs = key_ref.shape[0]
@@ -356,7 +350,6 @@
 
     project(
         token_ref[...],
-        weight_copy.wait,
         weight_ref,
         left_q_ref[...],
         right_q_ref[...],
@@ -499,12 +492,11 @@
 
     return pl.pallas_call(
         kernel,
-        in_specs=[smem] * 3 + [either] * (len(chunks) + len(ready) + 4) + [vmem] * len(operands),
+        in_specs=[smem] * 3 + [either] * (len(chunks) + len(ready) + 3) + [vmem] * (1 + len(operands)),
         out_specs=[vmem] * out_parts,
         out_shape=[jax.ShapeDtypeStruct((rows // out_parts, width), jnp.bfloat16)] * out_parts,
         scratch_shapes=[
             pltpu.VMEM((chunk_rows * len(chunks), width), jnp.bfloat16),
-            pltpu.VMEM(weight.shape, jnp.bfloat16),
             pltpu.VMEM(out_weight.shape, jnp.bfloat16),
             pltpu.VMEM(keys.shape, jnp.bfloat16),
             pltpu.VMEM(values.shape, jnp.bfloat16),
@@ -512,11 +504,11 @@
             pltpu.VMEM((qdim // LANES, rows, LANES), jnp.float32),
             pltpu.VMEM((LANES, width), jnp.bfloat16),
             pltpu.VMEM((group_rows, LANES), jnp.float32),
-            pltpu.SemaphoreType.DMA((4,)),
+            pltpu.SemaphoreType.DMA((3,)),
             pltpu.SemaphoreType.DMA((len(chunks) + len(ready),)),
         ],
-        compiler_params=pltpu.CompilerParams(vmem_limit_bytes=57 * 1024 * 1024),
-    )(lengths, sinks, place, *chunks, *ready, weight, out_weight, keys, values, *operands)
+        compiler_params=pltpu.CompilerParams(vmem_limit_bytes=38 * 1024 * 1024),
+    )(lengths, sinks, place, *chunks, *ready, out_weight, keys, values, weight, *operands)
 
 
 def shards(
@@ -566,8 +558,6 @@
         held[0], held[1] = mine, lax.ppermute(mine, "member", pairs)
         return after
 
-    keys, values = relayout(key_cache[0, 0], value_cache[0, 0])
-
     offsets = [0]
     for distance in range(1, ring // 2):
         offsets += [distance, -distance]
@@ -590,17 +580,22 @@
     half = own.shape[0] // 2
     exchange(member_count // 2, ())
     from_left, from_right = [own, to_right(own)], [own, to_left(own)]
-    keys, values, cosines, sines, onward, back = lax.optimization_barrier(
-        (keys, values, cosines, sines, from_left[1], from_right[1])
+    cosines, sines, onward, back = lax.optimization_barrier(
+        (cosines, sines, from_left[1], from_right[1])
     )
     from_left.append(to_right(onward))
     from_right.append(to_left(back))
     exchange(member_count // 4, from_left[1])
+    cached = lax.optimization_barrier((key_cache, value_cache, onward))
+    keys, values = relayout(cached[0][0, 0], cached[1][0, 0])
     own_rows = own.shape[0]
     factor_operands = (flat_weight, query_left[0], query_right[0], cosines, sines)
     for distance in range(3, ring // 2):
-        from_left.append(to_right(from_left[-1]))
-        from_right.append(to_left(from_right[-1]))
+        keys, values, onward, back = lax.optimization_barrier(
+            (keys, values, from_left[-1], from_right[-1])
+        )
+        from_left.append(to_right(onward))
+        from_right.append(to_left(back))
     near = [own]
     for distance in range(1, ring // 2):
         near += [from_right[distance], from_left[distance]]
@@ -648,26 +643,35 @@
         output_master,
     )
 
-    results = []
-    for k in range(2):
-        at = {offset: shares[2 * i + k] for i, offset in enumerate(offsets)}
-
-        def plus(received, offset):
-            return (received.astype(jnp.float32) + at[offset].astype(jnp.float32)).astype(
+    at = {
+        (offset, k): shares[2 * i + k] for i, offset in enumerate(offsets) for k in range(2)
+    }
+    last = ring // 2 - 1
+    chains = [
+        dict(way=to_right, sign=1, k=0, next=last, moving=at[last + 1, 0]),
+        dict(way=to_left, sign=-1, k=1, next=last, moving=at[last + 1, 1]),
+        dict(way=to_left, sign=-1, k=0, next=last - 1, moving=at[-last, 0]),
+        dict(way=to_right, sign=1, k=1, next=last - 1, moving=at[last, 1]),
+    ]
+    before = None
+    for chain in chains:
+        chain["moving"] = chain["way"](chain["moving"])
+    for _ in range(last):
+        for chain in chains:
+            if chain["next"] == 0:
+                continue
+            mine = at[chain["sign"] * chain["next"], chain["k"]]
+            if before is not None:
+                mine, before = lax.optimization_barrier((mine, before))
+            before = (chain["moving"].astype(jnp.float32) + mine.astype(jnp.float32)).astype(
                 jnp.bfloat16
             )
-
-        last = ring // 2 - 1
-        if k == 0:
-            rightward = plus(to_right(at[last + 1]), last)
-            leftward = at[-last]
-        else:
-            rightward = at[last]
-            leftward = plus(to_left(at[last + 1]), -last)
-        for distance in range(last - 1, 0, -1):
-            rightward = plus(to_right(rightward), distance)
-            leftward = plus(to_left(leftward), -distance)
-        results.append((to_right(rightward), to_left(leftward), at[0]))
+            chain["moving"] = chain["way"](before)
+            chain["next"] -= 1
+    results = [
+        (chains[0]["moving"], chains[2]["moving"], at[0, 0]),
+        (chains[3]["moving"], chains[1]["moving"], at[0, 1]),
+    ]
     mine, updated = lax.optimization_barrier(([r[2] for r in results], tuple(updated)))
     layer_output = []
     for (from_left, from_right, _), own_share in zip(results, mine):

time: 113 us -> 104 us (0.920)
  Pallas kernels: 38.7 us -> 27.9 us
  starting transfers between devices: 45.8 us -> 37.2 us
  waiting for transfers between devices: 18.4 us -> 25.8 us
  other arithmetic: 5.98 us -> 8.06 us
  local copies, waits for them, and re-layouts: 1.83 us -> 3.05 us
    ppermute x11, starting transfers between devices: 35.4 us -> 20.4 us  [to_left(): return lax.ppermute(x, 'head', left_pairs)]
    ppermute x11, waiting for transfers between devices: 4.78 us -> 13 us  [to_right(): return lax.ppermute(x, 'head', right_pairs)]
    ppermute x11, starting transfers between devices: 2.68 us -> 10 us  [to_right(): return lax.ppermute(x, 'head', right_pairs)]
    pallas_call x2, Pallas kernels: 12.4 us -> 6.07 us  [project_chunks(): pl.pallas_call(kernel, in_specs=[either] * len(chunks) + [vmem] * 5, out_...]
    pallas_call x1, Pallas kernels: 18.6 us -> 14 us  [layer(): pl.pallas_call(kernel, in_specs=[smem] * 3 + [either] * (len(chunks) + le...]
    concatenate x4, other arithmetic: 0.13 us -> 1.83 us  [exchange(): mine = jnp.concatenate(held, axis=0)]
    unnamed x46 -> x42, local copies, waits for them, and re-layouts: 0.81 us -> 2.04 us
  transfers between devices with their start and end apart: 27 -> 27, of which waited for: 5 -> 12; matrix products, arithmetic and copies ran while one was open for 5% -> 8% of each run, Pallas kernels for 34% -> 27%
where the time goes in v1:
time: 104 us
  starting transfers between devices  37.2 us (36%)
  Pallas kernels  27.9 us (27%)
  waiting for transfers between devices  25.8 us (25%)
  other arithmetic  8.06 us (8%)
  local copies, waits for them, and re-layouts  3.05 us (3%)
  between operations  1.72 us (2%)
    ppermute x11, starting transfers between devices, to_left(): return lax.ppermute(x, 'head', left_pairs)  20.4 us
    pallas_call x1, Pallas kernels, layer(): pl.pallas_call(kernel, in_specs=[smem] * 3 + [either] * (len(chunks) + le...  14 us
    ppermute x11, waiting for transfers between devices, to_right(): return lax.ppermute(x, 'head', right_pairs)  13 us
    ppermute x11, waiting for transfers between devices, to_left(): return lax.ppermute(x, 'head', left_pairs)  12.8 us
    ppermute x11, starting transfers between devices, to_right(): return lax.ppermute(x, 'head', right_pairs)  10 us
    ppermute x5, starting transfers between devices, exchange(): held[0], held[1] = (mine, lax.ppermute(mine, 'member', pairs))  6.81 us
    pallas_call x2, Pallas kernels, project_chunks(): pl.pallas_call(kernel, in_specs=[either] * len(chunks) + [vmem] * 5, out_...  6.07 us
    pallas_call x1, Pallas kernels, relayout(): pl.pallas_call(relayout_kernel, in_specs=[hbm] * 2, out_specs=[hbm] * 2,...  5.14 us
  transfers between devices with their start and end apart: 27, of which 12 were waited for; matrix products, arithmetic and copies ran while one was open for 8% of the time, Pallas kernels for 27%

profile of v1, /device:TPU:8, one launch (start us, length us, event | category | flops | bytes accessed | tf_op | source)
XLA Modules:
  0.0 103.7 jit_solution(9820863590343594872)
XLA Ops:
  0.6 2.0 %collective-permute-start.1 = (bf16[64,2880]{1,0:T(8,128)(2,1)}, bf16[64,2880]{1,0:T(8,128)(2,1)}, u32[]{:S(2)}, u32[]{:S(2)}) collective-permute-start(bf16[64,2880]{1,0:T(8,128)(2,1)} %bitcast.26), channel_id=1, source_target_pairs={{0,1},{1,2},{2,3},{3,4},{4,5},{5,6},{6,7},{7,0},{8,9},{9,10},{10,1... | collective-permute-start | bytes 1105928 | tf_op jit(solution)/shard_map/ppermute | solution.py:538
  2.6 4.0 %collective-permute-start = (bf16[64,2880]{1,0:T(8,128)(2,1)}, bf16[64,2880]{1,0:T(8,128)(2,1)}, u32[]{:S(2)}, u32[]{:S(2)}) collective-permute-start(bf16[64,2880]{1,0:T(8,128)(2,1)} %bitcast.27), channel_id=1, source_target_pairs={{0,7},{1,0},{2,1},{3,2},{4,3},{5,4},{6,5},{7,6},{8,15},{9,8},{10,9... | collective-permute-start | bytes 1105928 | tf_op jit(solution)/shard_map/ppermute | solution.py:541
  7.3 1.5 %shard_map.204 = bf16[8,3456]{1,0:T(8,128)(2,1)} custom-call(f32[1]{0:T(128)S(6)} %copy.22.fitness_ref, f32[4,2880]{1,0:T(4,128)} %bitcast.22, f32[4,2880]{1,0:T(4,128)} %bitcast.29, f32[4,512]{1,0:T(4,128)} %bitcast.31, f32[4,512]{1,0:T(4,128)} %bitcast.35), custom_call_target="tpu_custom_call" | custom-call | tf_op jit(solution)/shard_map/pallas_call | solution.py:97
  8.8 2.3 %collective-permute-start.19 = (bf16[8,3456]{1,0:T(8,128)(2,1)}, bf16[8,3456]{1,0:T(8,128)(2,1)S(1)}, u32[]{:S(2)}, u32[]{:S(2)}) collective-permute-start(bf16[8,3456]{1,0:T(8,128)(2,1)} %shard_map.204), channel_id=1, source_target_pairs={{0,128},{8,136},{16,144},{24,152},{32,160},{40,168},{48,176},{56,1... | collective-permute-start | bytes 165896 | tf_op jit(solution)/shard_map/ppermute | solution.py:558
  12.8 1.8 %fusion = (f32[512,128]{1,0:T(8,128)S(1)}, f32[512,128]{1,0:T(8,128)}) fusion(f32[128]{0:T(128)S(1)} %get-tuple-element.115, f32[128]{0:T(128)S(1)} %get-tuple-element.116, f32[512]{0:T(512)S(1)} %add_convert_fusion.12), kind=kLoop, calls=%fused_computation.17 | loop fusion | flops 131072 | bytes 527360 | tf_op jit(solution)/shard_map/mul | solution.py:577
  15.6 3.0 %collective-permute-start.2 = (bf16[64,2880]{1,0:T(8,128)(2,1)}, bf16[64,2880]{1,0:T(8,128)(2,1)}, u32[]{:S(2)}, u32[]{:S(2)}) collective-permute-start(bf16[64,2880]{1,0:T(8,128)(2,1)} %collective-permute-done.refs_1_), channel_id=1, source_target_pairs={{0,7},{1,0},{2,1},{3,2},{4,3},{5,4},{6,5},{7,6},{8,15},{9,8},{10,9... | collective-permute-start | bytes 1105928 | tf_op jit(solution)/shard_map/ppermute | solution.py:541
  20.0 5.1 %shard_map.201 = (bf16[16,512,128]{2,1,0:T(8,128)(2,1)}, bf16[16,512,128]{2,1,0:T(8,128)(2,1)}) custom-call(bf16[16,65536]{1,0:T(8,128)(2,1)} %bitcast.39, bf16[16,65536]{1,0:T(8,128)(2,1)} %bitcast.40), custom_call_target="tpu_custom_call" | custom-call | tf_op jit(solution)/shard_map/pallas_call | solution.py:67
  26.2 3.4 %collective-permute-done.3.refs_4_ = bf16[64,2880]{1,0:T(8,128)(2,1)} collective-permute-done((bf16[64,2880]{1,0:T(8,128)(2,1)}, bf16[64,2880]{1,0:T(8,128)(2,1)}, u32[]{:S(2)}, u32[]{:S(2)}) %collective-permute-start.3) | collective-permute-done | bytes 368672 | tf_op jit(solution)/shard_map/ppermute | solution.py:538
  29.6 3.2 %collective-permute-start.5 = (bf16[64,2880]{1,0:T(8,128)(2,1)}, bf16[64,2880]{1,0:T(8,128)(2,1)S(1)}, u32[]{:S(2)}, u32[]{:S(2)}) collective-permute-start(bf16[64,2880]{1,0:T(8,128)(2,1)} %collective-permute-done.2.refs_3_), channel_id=1, source_target_pairs={{0,7},{1,0},{2,1},{3,2},{4,3},{5,4},{6,5},{7,6},{8,15},{9,8},{10,9... | collective-permute-start | bytes 1105928 | tf_op jit(solution)/shard_map/ppermute | solution.py:541
  33.7 3.3 %collective-permute-start.21 = (bf16[32,3456]{1,0:T(8,128)(2,1)S(1)}, bf16[32,3456]{1,0:T(8,128)(2,1)S(1)}, u32[]{:S(2)}, u32[]{:S(2)}) collective-permute-start(bf16[32,3456]{1,0:T(8,128)(2,1)S(1)} %pad_maximum_fusion.2), channel_id=1, source_target_pairs={{0,32},{8,40},{16,48},{24,56},{32,0},{40,8},{48,16},{56,24},{64,96... | collective-permute-start | bytes 663560 | tf_op jit(solution)/shard_map/ppermute | solution.py:558
  39.0 4.1 %shard_map.200.refs_5_ = f32[5,320,128]{2,1,0:T(8,128)S(1)} custom-call(bf16[64,2880]{1,0:T(8,128)(2,1)S(1)} %bitcast.28, bf16[64,2880]{1,0:T(8,128)(2,1)} %collective-permute-done.refs_1_, bf16[64,2880]{1,0:T(8,128)(2,1)} %collective-permute-done.1.refs_2_, bf16[64,2880]{1,0:T(8,128)(2,1)} %collective-permute-done.2.refs_3_, ...), custom_call_target="tpu_custom_call" | custom-call | tf_op jit(solution)/shard_map/pallas_call | solution.py:266
  43.3 3.2 %collective-permute-start.7 = (bf16[32,2880]{1,0:T(8,128)(2,1)S(1)}, bf16[32,2880]{1,0:T(8,128)(2,1)S(1)}, u32[]{:S(2)}, u32[]{:S(2)}) collective-permute-start(bf16[32,2880]{1,0:T(8,128)(2,1)S(1)} %slice.9), channel_id=1, source_target_pairs={{0,7},{1,0},{2,1},{3,2},{4,3},{5,4},{6,5},{7,6},{8,15},{9,8},{10,9... | collective-permute-start | bytes 552968 | tf_op jit(solution)/shard_map/ppermute | solution.py:541
  46.6 2.0 %shard_map.202.refs_6_ = f32[5,128,128]{2,1,0:T(8,128)S(1)} custom-call(bf16[64,2880]{1,0:T(8,128)(2,1)S(1)} %collective-permute-done.5.refs_0_, bf16[64,2880]{1,0:T(8,128)(2,1)S(1)} %collective-permute-done.4.refs_1_, bf16[2880,640]{1,0:T(8,128)(2,1)S(1)} %bitcast.19, f32[4,2880]{1,0:T(4,128)S(1)} %bitcast.24, f32[4,512]{1,0:T(4,128)S(1)} %bitcast.33, ...), custom_call_target="tpu_custom_call" | custom-call | tf_op jit(solution)/shard_map/pallas_call | solution.py:266
  48.5 1.6 %collective-permute-done.6.refs_3_ = bf16[32,2880]{1,0:T(8,128)(2,1)S(1)} collective-permute-done((bf16[32,2880]{1,0:T(8,128)(2,1)S(1)}, bf16[32,2880]{1,0:T(8,128)(2,1)S(1)}, u32[]{:S(2)}, u32[]{:S(2)}) %collective-permute-start.6) | collective-permute-done | bytes 184352 | tf_op jit(solution)/shard_map/ppermute | solution.py:538
  50.2 14.0 %shard_map.203 = (bf16[32,2880]{1,0:T(8,128)(2,1)S(1)}, bf16[32,2880]{1,0:T(8,128)(2,1)S(1)}, bf16[32,2880]{1,0:T(8,128)(2,1)S(1)}, bf16[32,2880]{1,0:T(8,128)(2...) custom-call(s32[16]{0:T(128)S(1)} %bitcast.38, ...), custom_call_target="tpu_custom_call" | custom-call | tf_op jit(solution)/shard_map/pallas_call | solution.py:493
  65.0 2.3 %collective-permute-start.10 = (bf16[32,2880]{1,0:T(8,128)(2,1)S(1)}, bf16[32,2880]{1,0:T(8,128)(2,1)S(1)}, u32[]{:S(2)}, u32[]{:S(2)}) collective-permute-start(bf16[32,2880]{1,0:T(8,128)(2,1)S(1)} %get-tuple-element.77), channel_id=1, source_target_pairs={{0,1},{1,2},{2,3},{3,4},{4,5},{5,6},{6,7},{7,0},{8,9},{9,10},{10,1... | collective-permute-start | bytes 552968 | tf_op jit(solution)/shard_map/ppermute | solution.py:538
  68.3 2.0 %collective-permute-start.12 = (bf16[32,2880]{1,0:T(8,128)(2,1)S(1)}, bf16[32,2880]{1,0:T(8,128)(2,1)S(1)}, u32[]{:S(2)}, u32[]{:S(2)}) collective-permute-start(bf16[32,2880]{1,0:T(8,128)(2,1)S(1)} %get-tuple-element.81), channel_id=1, source_target_pairs={{0,7},{1,0},{2,1},{3,2},{4,3},{5,4},{6,5},{7,6},{8,15},{9,8},{10,9... | collective-permute-start | bytes 552968 | tf_op jit(solution)/shard_map/ppermute | solution.py:541
  70.3 2.3 %collective-permute-done.8 = bf16[32,2880]{1,0:T(8,128)(2,1)S(1)} collective-permute-done((bf16[32,2880]{1,0:T(8,128)(2,1)S(1)}, bf16[32,2880]{1,0:T(8,128)(2,1)S(1)}, u32[]{:S(2)}, u32[]{:S(2)}) %collective-permute-start.8) | collective-permute-done | bytes 184352 | tf_op jit(solution)/shard_map/ppermute | solution.py:538
  72.7 7.0 %collective-permute-done.12 = bf16[32,2880]{1,0:T(8,128)(2,1)S(1)} collective-permute-done((bf16[32,2880]{1,0:T(8,128)(2,1)S(1)}, bf16[32,2880]{1,0:T(8,128)(2,1)S(1)}, u32[]{:S(2)}, u32[]{:S(2)}) %collective-permute-start.12) | collective-permute-done | bytes 184352 | tf_op jit(solution)/shard_map/ppermute | solution.py:541
  82.7 2.1 %collective-permute-start.13 = (bf16[32,2880]{1,0:T(8,128)(2,1)S(1)}, bf16[32,2880]{1,0:T(8,128)(2,1)S(1)}, u32[]{:S(2)}, u32[]{:S(2)}) collective-permute-start(bf16[32,2880]{1,0:T(8,128)(2,1)S(1)} %add_convert_fusion.7), channel_id=1, source_target_pairs={{0,1},{1,2},{2,3},{3,4},{4,5},{5,6},{6,7},{7,0},{8,9},{9,10},{10,1... | collective-permute-start | bytes 552968 | tf_op jit(solution)/shard_map/ppermute | solution.py:538
  87.7 1.7 %collective-permute-done.14 = bf16[32,2880]{1,0:T(8,128)(2,1)S(1)} collective-permute-done((bf16[32,2880]{1,0:T(8,128)(2,1)S(1)}, bf16[32,2880]{1,0:T(8,128)(2,1)S(1)}, u32[]{:S(2)}, u32[]{:S(2)}) %collective-permute-start.14) | collective-permute-done | bytes 184352 | tf_op jit(solution)/shard_map/ppermute | solution.py:538
  90.5 2.9 %collective-permute-done.13 = bf16[32,2880]{1,0:T(8,128)(2,1)S(1)} collective-permute-done((bf16[32,2880]{1,0:T(8,128)(2,1)S(1)}, bf16[32,2880]{1,0:T(8,128)(2,1)S(1)}, u32[]{:S(2)}, u32[]{:S(2)}) %collective-permute-start.13) | collective-permute-done | bytes 184352 | tf_op jit(solution)/shard_map/ppermute | solution.py:538
  95.6 2.0 %collective-permute-start.17 = (bf16[32,2880]{1,0:T(8,128)(2,1)S(1)}, bf16[32,2880]{1,0:T(8,128)(2,1)S(1)}, u32[]{:S(2)}, u32[]{:S(2)}) collective-permute-start(bf16[32,2880]{1,0:T(8,128)(2,1)S(1)} %add_convert_fusion.3), channel_id=1, source_target_pairs={{0,1},{1,2},{2,3},{3,4},{4,5},{5,6},{6,7},{7,0},{8,9},{9,10},{10,1... | collective-permute-start | bytes 552968 | tf_op jit(solution)/shard_map/ppermute | solution.py:538
  98.8 2.1 %collective-permute-done.26 = bf16[32,2880]{1,0:T(8,128)(2,1)} collective-permute-done((bf16[32,2880]{1,0:T(8,128)(2,1)}, bf16[32,2880]{1,0:T(8,128)(2,1)}, u32[]{:S(2)}, u32[]{:S(2)}) %collective-permute-start.26) | collective-permute-done | bytes 184352 | tf_op jit(solution)/shard_map/ppermute | solution.py:541
  (107 shorter events, 23.1 us)
Async XLA Ops:
  0.6 15.0 %collective-permute-start.1 = (bf16[64,2880]{1,0:T(8,128)(2,1)}, bf16[64,2880]{1,0:T(8,128)(2,1)}, u32[]{:S(2)}, u32[]{:S(2)}) collective-permute-start(bf16[64,2880]{1,0:T(8,128)(2,1)} %bitcast.26), channel_id=1, source_target_pairs={{0,1},{1,2},{2,3},{3,4},{4,5},{5,6},{6,7},{7,0},{8,9},{9,10},{10,1... | collective-permute-start | bytes 1105928 | tf_op jit(solution)/shard_map/ppermute | solution.py:538
  2.6 13.0 %collective-permute-start = (bf16[64,2880]{1,0:T(8,128)(2,1)}, bf16[64,2880]{1,0:T(8,128)(2,1)}, u32[]{:S(2)}, u32[]{:S(2)}) collective-permute-start(bf16[64,2880]{1,0:T(8,128)(2,1)} %bitcast.27), channel_id=1, source_target_pairs={{0,7},{1,0},{2,1},{3,2},{4,3},{5,4},{6,5},{7,6},{8,15},{9,8},{10,9... | collective-permute-start | bytes 1105928 | tf_op jit(solution)/shard_map/ppermute | solution.py:541
  8.8 9.9 %collective-permute-start.19 = (bf16[8,3456]{1,0:T(8,128)(2,1)}, bf16[8,3456]{1,0:T(8,128)(2,1)S(1)}, u32[]{:S(2)}, u32[]{:S(2)}) collective-permute-start(bf16[8,3456]{1,0:T(8,128)(2,1)} %shard_map.204), channel_id=1, source_target_pairs={{0,128},{8,136},{16,144},{24,152},{32,160},{40,168},{48,176},{56,1... | collective-permute-start | bytes 165896 | tf_op jit(solution)/shard_map/ppermute | solution.py:558
  15.6 10.5 %collective-permute-start.2 = (bf16[64,2880]{1,0:T(8,128)(2,1)}, bf16[64,2880]{1,0:T(8,128)(2,1)}, u32[]{:S(2)}, u32[]{:S(2)}) collective-permute-start(bf16[64,2880]{1,0:T(8,128)(2,1)} %collective-permute-done.refs_1_), channel_id=1, source_target_pairs={{0,7},{1,0},{2,1},{3,2},{4,3},{5,4},{6,5},{7,6},{8,15},{9,8},{10,9... | collective-permute-start | bytes 1105928 | tf_op jit(solution)/shard_map/ppermute | solution.py:541
  18.7 10.9 %collective-permute-start.3 = (bf16[64,2880]{1,0:T(8,128)(2,1)}, bf16[64,2880]{1,0:T(8,128)(2,1)}, u32[]{:S(2)}, u32[]{:S(2)}) collective-permute-start(bf16[64,2880]{1,0:T(8,128)(2,1)} %collective-permute-done.1.refs_2_), channel_id=1, source_target_pairs={{0,1},{1,2},{2,3},{3,4},{4,5},{5,6},{6,7},{7,0},{8,9},{9,10},{10,1... | collective-permute-start | bytes 1105928 | tf_op jit(solution)/shard_map/ppermute | solution.py:538
  19.5 13.3 %collective-permute-start.20 = (bf16[16,3456]{1,0:T(8,128)(2,1)S(1)}, bf16[16,3456]{1,0:T(8,128)(2,1)}, u32[]{:S(2)}, u32[]{:S(2)}) collective-permute-start(bf16[16,3456]{1,0:T(8,128)(2,1)S(1)} %pad_maximum_fusion.3), channel_id=1, source_target_pairs={{0,64},{8,72},{16,80},{24,88},{32,96},{40,104},{48,112},{56,120},{... | collective-permute-start | bytes 331784 | tf_op jit(solution)/shard_map/ppermute | solution.py:558
  29.6 13.5 %collective-permute-start.4 = (bf16[64,2880]{1,0:T(8,128)(2,1)}, bf16[64,2880]{1,0:T(8,128)(2,1)S(1)}, u32[]{:S(2)}, u32[]{:S(2)}) collective-permute-start(bf16[64,2880]{1,0:T(8,128)(2,1)} %collective-permute-done.3.refs_4_), channel_id=1, source_target_pairs={{0,1},{1,2},{2,3},{3,4},{4,5},{5,6},{6,7},{7,0},{8,9},{9,10},{10,1... | collective-permute-start | bytes 1105928 | tf_op jit(solution)/shard_map/ppermute | solution.py:538
  29.6 13.6 %collective-permute-start.5 = (bf16[64,2880]{1,0:T(8,128)(2,1)}, bf16[64,2880]{1,0:T(8,128)(2,1)S(1)}, u32[]{:S(2)}, u32[]{:S(2)}) collective-permute-start(bf16[64,2880]{1,0:T(8,128)(2,1)} %collective-permute-done.2.refs_3_), channel_id=1, source_target_pairs={{0,7},{1,0},{2,1},{3,2},{4,3},{5,4},{6,5},{7,6},{8,15},{9,8},{10,9... | collective-permute-start | bytes 1105928 | tf_op jit(solution)/shard_map/ppermute | solution.py:541
  33.7 30.6 %collective-permute-start.21 = (bf16[32,3456]{1,0:T(8,128)(2,1)S(1)}, bf16[32,3456]{1,0:T(8,128)(2,1)S(1)}, u32[]{:S(2)}, u32[]{:S(2)}) collective-permute-start(bf16[32,3456]{1,0:T(8,128)(2,1)S(1)} %pad_maximum_fusion.2), channel_id=1, source_target_pairs={{0,32},{8,40},{16,48},{24,56},{32,0},{40,8},{48,16},{56,24},{64,96... | collective-permute-start | bytes 663560 | tf_op jit(solution)/shard_map/ppermute | solution.py:558
  43.2 6.9 %collective-permute-start.6 = (bf16[32,2880]{1,0:T(8,128)(2,1)S(1)}, bf16[32,2880]{1,0:T(8,128)(2,1)S(1)}, u32[]{:S(2)}, u32[]{:S(2)}) collective-permute-start(bf16[32,2880]{1,0:T(8,128)(2,1)S(1)} %slice.8), channel_id=1, source_target_pairs={{0,1},{1,2},{2,3},{3,4},{4,5},{5,6},{6,7},{7,0},{8,9},{9,10},{10,1... | collective-permute-start | bytes 552968 | tf_op jit(solution)/shard_map/ppermute | solution.py:538
  64.2 8.4 %collective-permute-start.8 = (bf16[32,2880]{1,0:T(8,128)(2,1)S(1)}, bf16[32,2880]{1,0:T(8,128)(2,1)S(1)}, u32[]{:S(2)}, u32[]{:S(2)}) collective-permute-start(bf16[32,2880]{1,0:T(8,128)(2,1)S(1)} %get-tuple-element.74), channel_id=1, source_target_pairs={{0,1},{1,2},{2,3},{3,4},{4,5},{5,6},{6,7},{7,0},{8,9},{9,10},{10,1... | collective-permute-start | bytes 552968 | tf_op jit(solution)/shard_map/ppermute | solution.py:538
  64.3 18.1 %collective-permute-start.22 = (bf16[64,3456]{1,0:T(8,128)(2,1)S(1)}, bf16[64,3456]{1,0:T(8,128)(2,1)S(1)}, u32[]{:S(2)}, u32[]{:S(2)}) collective-permute-start(bf16[64,3456]{1,0:T(8,128)(2,1)S(1)} %pad_maximum_fusion.1), channel_id=1, source_target_pairs={{0,16},{8,24},{16,0},{24,8},{32,48},{40,56},{48,32},{56,40},{64,80... | collective-permute-start | bytes 1327112 | tf_op jit(solution)/shard_map/ppermute | solution.py:558
  65.0 16.3 %collective-permute-start.10 = (bf16[32,2880]{1,0:T(8,128)(2,1)S(1)}, bf16[32,2880]{1,0:T(8,128)(2,1)S(1)}, u32[]{:S(2)}, u32[]{:S(2)}) collective-permute-start(bf16[32,2880]{1,0:T(8,128)(2,1)S(1)} %get-tuple-element.77), channel_id=1, source_target_pairs={{0,1},{1,2},{2,3},{3,4},{4,5},{5,6},{6,7},{7,0},{8,9},{9,10},{10,1... | collective-permute-start | bytes 552968 | tf_op jit(solution)/shard_map/ppermute | solution.py:538
  67.3 12.5 %collective-permute-start.11 = (bf16[32,2880]{1,0:T(8,128)(2,1)S(1)}, bf16[32,2880]{1,0:T(8,128)(2,1)S(1)}, u32[]{:S(2)}, u32[]{:S(2)}) collective-permute-start(bf16[32,2880]{1,0:T(8,128)(2,1)S(1)} %get-tuple-element.79), channel_id=1, source_target_pairs={{0,7},{1,0},{2,1},{3,2},{4,3},{5,4},{6,5},{7,6},{8,15},{9,8},{10,9... | collective-permute-start | bytes 552968 | tf_op jit(solution)/shard_map/ppermute | solution.py:541
  68.3 11.4 %collective-permute-start.12 = (bf16[32,2880]{1,0:T(8,128)(2,1)S(1)}, bf16[32,2880]{1,0:T(8,128)(2,1)S(1)}, u32[]{:S(2)}, u32[]{:S(2)}) collective-permute-start(bf16[32,2880]{1,0:T(8,128)(2,1)S(1)} %get-tuple-element.81), channel_id=1, source_target_pairs={{0,7},{1,0},{2,1},{3,2},{4,3},{5,4},{6,5},{7,6},{8,15},{9,8},{10,9... | collective-permute-start | bytes 552968 | tf_op jit(solution)/shard_map/ppermute | solution.py:541
  72.6 10.0 %collective-permute-start.9 = (bf16[32,2880]{1,0:T(8,128)(2,1)S(1)}, bf16[32,2880]{1,0:T(8,128)(2,1)S(1)}, u32[]{:S(2)}, u32[]{:S(2)}) collective-permute-start(bf16[32,2880]{1,0:T(8,128)(2,1)S(1)} %add_convert_fusion.11), channel_id=1, source_target_pairs={{0,1},{1,2},{2,3},{3,4},{4,5},{5,6},{6,7},{7,0},{8,9},{9,10},{10,1... | collective-permute-start | bytes 552968 | tf_op jit(solution)/shard_map/ppermute | solution.py:538
  79.9 7.7 %collective-permute-start.15 = (bf16[32,2880]{1,0:T(8,128)(2,1)S(1)}, bf16[32,2880]{1,0:T(8,128)(2,1)S(1)}, u32[]{:S(2)}, u32[]{:S(2)}) collective-permute-start(bf16[32,2880]{1,0:T(8,128)(2,1)S(1)} %add_convert_fusion.9), channel_id=1, source_target_pairs={{0,7},{1,0},{2,1},{3,2},{4,3},{5,4},{6,5},{7,6},{8,15},{9,8},{10,9... | collective-permute-start | bytes 552968 | tf_op jit(solution)/shard_map/ppermute | solution.py:541
  81.3 8.0 %collective-permute-start.14 = (bf16[32,2880]{1,0:T(8,128)(2,1)S(1)}, bf16[32,2880]{1,0:T(8,128)(2,1)S(1)}, u32[]{:S(2)}, u32[]{:S(2)}) collective-permute-start(bf16[32,2880]{1,0:T(8,128)(2,1)S(1)} %add_convert_fusion.8), channel_id=1, source_target_pairs={{0,1},{1,2},{2,3},{3,4},{4,5},{5,6},{6,7},{7,0},{8,9},{9,10},{10,1... | collective-permute-start | bytes 552968 | tf_op jit(solution)/shard_map/ppermute | solution.py:538
  82.5 15.0 %collective-permute-start.23 = (bf16[128,3456]{1,0:T(8,128)(2,1)S(1)}, bf16[128,3456]{1,0:T(8,128)(2,1)S(1)}, u32[]{:S(2)}, u32[]{:S(2)}) collective-permute-start(bf16[128,3456]{1,0:T(8,128)(2,1)S(1)} %pad_maximum_fusion.refs_1_), channel_id=1, source_target_pairs={{0,8},{8,0},{16,24},{24,16},{32,40},{40,32},{48,56},{56,48},{64,72... | collective-permute-start | bytes 2654216 | tf_op jit(solution)/shard_map/ppermute | solution.py:558
  82.7 10.7 %collective-permute-start.13 = (bf16[32,2880]{1,0:T(8,128)(2,1)S(1)}, bf16[32,2880]{1,0:T(8,128)(2,1)S(1)}, u32[]{:S(2)}, u32[]{:S(2)}) collective-permute-start(bf16[32,2880]{1,0:T(8,128)(2,1)S(1)} %add_convert_fusion.7), channel_id=1, source_target_pairs={{0,1},{1,2},{2,3},{3,4},{4,5},{5,6},{6,7},{7,0},{8,9},{9,10},{10,1... | collective-permute-start | bytes 552968 | tf_op jit(solution)/shard_map/ppermute | solution.py:538
  85.7 7.8 %collective-permute-start.25 = (bf16[32,2880]{1,0:T(8,128)(2,1)S(1)}, bf16[32,2880]{1,0:T(8,128)(2,1)S(1)}, u32[]{:S(2)}, u32[]{:S(2)}) collective-permute-start(bf16[32,2880]{1,0:T(8,128)(2,1)S(1)} %add_convert_fusion.6), channel_id=1, source_target_pairs={{0,7},{1,0},{2,1},{3,2},{4,3},{5,4},{6,5},{7,6},{8,15},{9,8},{10,9... | collective-permute-start | bytes 552968 | tf_op jit(solution)/shard_map/ppermute | solution.py:541
  90.1 8.7 %collective-permute-start.24 = (bf16[32,2880]{1,0:T(8,128)(2,1)}, bf16[32,2880]{1,0:T(8,128)(2,1)S(1)}, u32[]{:S(2)}, u32[]{:S(2)}) collective-permute-start(bf16[32,2880]{1,0:T(8,128)(2,1)} %add_convert_fusion.4), channel_id=1, source_target_pairs={{0,1},{1,2},{2,3},{3,4},{4,5},{5,6},{6,7},{7,0},{8,9},{9,10},{10,1... | collective-permute-start | bytes 552968 | tf_op jit(solution)/shard_map/ppermute | solution.py:538
  95.5 7.3 %collective-permute-start.18 = (bf16[32,2880]{1,0:T(8,128)(2,1)S(1)}, bf16[32,2880]{1,0:T(8,128)(2,1)S(1)}, u32[]{:S(2)}, u32[]{:S(2)}) collective-permute-start(bf16[32,2880]{1,0:T(8,128)(2,1)S(1)} %add_convert_fusion.5), channel_id=1, source_target_pairs={{0,7},{1,0},{2,1},{3,2},{4,3},{5,4},{6,5},{7,6},{8,15},{9,8},{10,9... | collective-permute-start | bytes 552968 | tf_op jit(solution)/shard_map/ppermute | solution.py:541
  95.6 7.3 %collective-permute-start.17 = (bf16[32,2880]{1,0:T(8,128)(2,1)S(1)}, bf16[32,2880]{1,0:T(8,128)(2,1)S(1)}, u32[]{:S(2)}, u32[]{:S(2)}) collective-permute-start(bf16[32,2880]{1,0:T(8,128)(2,1)S(1)} %add_convert_fusion.3), channel_id=1, source_target_pairs={{0,1},{1,2},{2,3},{3,4},{4,5},{5,6},{6,7},{7,0},{8,9},{9,10},{10,1... | collective-permute-start | bytes 552968 | tf_op jit(solution)/shard_map/ppermute | solution.py:538
  (24 other events, 254.8 us)

commit v2 on v1

--- a/solution.py
+++ b/solution.py
@@ -608,6 +608,7 @@
     far = [to_right(onward), to_left(back)]
     second_projected = project_chunks(near[early:], early * own_rows, *factor_operands)
     exchange(member_count // 16, from_left[-1])
+    held[0], far[0] = lax.optimization_barrier((held[0], far[0]))
     projected = [first_projected, second_projected]
     shares = layer(
         lengths[0],

time: 104 us -> 104 us (level)
    ppermute x11, starting transfers between devices: 10 us -> 4.8 us  [to_right(): return lax.ppermute(x, 'head', right_pairs)]
    ppermute x11, starting transfers between devices: 20.4 us -> 25.2 us  [to_left(): return lax.ppermute(x, 'head', left_pairs)]
    ppermute x11, waiting for transfers between devices: 13 us -> 16.1 us  [to_right(): return lax.ppermute(x, 'head', right_pairs)]
    ppermute x11, waiting for transfers between devices: 12.8 us -> 9.82 us  [to_left(): return lax.ppermute(x, 'head', left_pairs)]
  transfers between devices with their start and end apart: 27 -> 27, of which waited for: 12 -> 12; matrix products, arithmetic and copies ran while one was open for 8% -> 8% of each run, Pallas kernels for 27% -> 13%
where the time goes in v2:
time: 104 us; the launch traced here: 103 us
  starting transfers between devices  36.8 us (35%)
  Pallas kernels  27.9 us (27%)
  waiting for transfers between devices  25.9 us (25%)
  other arithmetic  8.07 us (8%)
  local copies, waits for them, and re-layouts  3.05 us (3%)
  between operations  1.7 us (2%)
    ppermute x11, starting transfers between devices, to_left(): return lax.ppermute(x, 'head', left_pairs)  25.2 us
    ppermute x11, waiting for transfers between devices, to_right(): return lax.ppermute(x, 'head', right_pairs)  16.1 us
    pallas_call x1, Pallas kernels, layer(): pl.pallas_call(kernel, in_specs=[smem] * 3 + [either] * (len(chunks) + le...  14 us
    ppermute x11, waiting for transfers between devices, to_left(): return lax.ppermute(x, 'head', left_pairs)  9.82 us
    ppermute x5, starting transfers between devices, exchange(): held[0], held[1] = (mine, lax.ppermute(mine, 'member', pairs))  6.8 us
    pallas_call x2, Pallas kernels, project_chunks(): pl.pallas_call(kernel, in_specs=[either] * len(chunks) + [vmem] * 5, out_...  6.08 us
    pallas_call x1, Pallas kernels, relayout(): pl.pallas_call(relayout_kernel, in_specs=[hbm] * 2, out_specs=[hbm] * 2,...  5.14 us
    ppermute x11, starting transfers between devices, to_right(): return lax.ppermute(x, 'head', right_pairs)  4.8 us
  transfers between devices with their start and end apart: 27, of which 12 were waited for; matrix products, arithmetic and copies ran while one was open for 8% of the time, Pallas kernels for 13%

profile of v2, /device:TPU:8, one launch (start us, length us, event | category | flops | bytes accessed | tf_op | source)
XLA Modules:
  0.0 103.4 jit_solution(16508891607076914085)
XLA Ops:
  0.6 5.9 %collective-permute-start.3 = (bf16[64,2880]{1,0:T(8,128)(2,1)}, bf16[64,2880]{1,0:T(8,128)(2,1)}, u32[]{:S(2)}, u32[]{:S(2)}) collective-permute-start(bf16[64,2880]{1,0:T(8,128)(2,1)} %bitcast.26), channel_id=1, source_target_pairs={{0,7},{1,0},{2,1},{3,2},{4,3},{5,4},{6,5},{7,6},{8,15},{9,8},{10,9... | collective-permute-start | bytes 1105928 | tf_op jit(solution)/shard_map/ppermute | solution.py:541
  8.7 2.3 %collective-permute-start = (bf16[8,3456]{1,0:T(8,128)(2,1)}, bf16[8,3456]{1,0:T(8,128)(2,1)S(1)}, u32[]{:S(2)}, u32[]{:S(2)}) collective-permute-start(bf16[8,3456]{1,0:T(8,128)(2,1)} %shard_map.200), channel_id=1, source_target_pairs={{0,128},{8,136},{16,144},{24,152},{32,160},{40,168},{48,176},{56,1... | collective-permute-start | bytes 165896 | tf_op jit(solution)/shard_map/ppermute | solution.py:558
  12.7 1.8 %fusion = (f32[512,128]{1,0:T(8,128)S(1)}, f32[512,128]{1,0:T(8,128)}) fusion(f32[128]{0:T(128)S(1)} %get-tuple-element.119, f32[128]{0:T(128)S(1)} %get-tuple-element.120, f32[512]{0:T(512)S(1)} %add_convert_fusion.12), kind=kLoop, calls=%fused_computation.17 | loop fusion | flops 131072 | bytes 527360 | tf_op jit(solution)/shard_map/mul | solution.py:577
  14.9 3.4 %collective-permute-done.1.refs_2_ = bf16[64,2880]{1,0:T(8,128)(2,1)} collective-permute-done((bf16[64,2880]{1,0:T(8,128)(2,1)}, bf16[64,2880]{1,0:T(8,128)(2,1)}, u32[]{:S(2)}, u32[]{:S(2)}) %collective-permute-start.1) | collective-permute-done | bytes 368672 | tf_op jit(solution)/shard_map/ppermute | solution.py:538
  18.6 1.7 %collective-permute-start.4 = (bf16[64,2880]{1,0:T(8,128)(2,1)}, bf16[64,2880]{1,0:T(8,128)(2,1)}, u32[]{:S(2)}, u32[]{:S(2)}) collective-permute-start(bf16[64,2880]{1,0:T(8,128)(2,1)} %collective-permute-done.1.refs_2_), channel_id=1, source_target_pairs={{0,1},{1,2},{2,3},{3,4},{4,5},{5,6},{6,7},{7,0},{8,9},{9,10},{10,1... | collective-permute-start | bytes 1105928 | tf_op jit(solution)/shard_map/ppermute | solution.py:538
  21.6 5.1 %shard_map.201 = (bf16[16,512,128]{2,1,0:T(8,128)(2,1)}, bf16[16,512,128]{2,1,0:T(8,128)(2,1)}) custom-call(bf16[16,65536]{1,0:T(8,128)(2,1)} %bitcast.39, bf16[16,65536]{1,0:T(8,128)(2,1)} %bitcast.40), custom_call_target="tpu_custom_call" | custom-call | tf_op jit(solution)/shard_map/pallas_call | solution.py:67
  27.9 1.5 %collective-permute-done.4.refs_4_ = bf16[64,2880]{1,0:T(8,128)(2,1)} collective-permute-done((bf16[64,2880]{1,0:T(8,128)(2,1)}, bf16[64,2880]{1,0:T(8,128)(2,1)}, u32[]{:S(2)}, u32[]{:S(2)}) %collective-permute-start.4) | collective-permute-done | bytes 368672 | tf_op jit(solution)/shard_map/ppermute | solution.py:538
  29.7 3.0 %collective-permute-start.8 = (bf16[64,2880]{1,0:T(8,128)(2,1)}, bf16[64,2880]{1,0:T(8,128)(2,1)S(1)}, u32[]{:S(2)}, u32[]{:S(2)}) collective-permute-start(bf16[64,2880]{1,0:T(8,128)(2,1)} %collective-permute-done.6.refs_3_), channel_id=1, source_target_pairs={{0,7},{1,0},{2,1},{3,2},{4,3},{5,4},{6,5},{7,6},{8,15},{9,8},{10,9... | collective-permute-start | bytes 1105928 | tf_op jit(solution)/shard_map/ppermute | solution.py:541
  33.6 3.3 %collective-permute-start.5 = (bf16[32,3456]{1,0:T(8,128)(2,1)S(1)}, bf16[32,3456]{1,0:T(8,128)(2,1)S(1)}, u32[]{:S(2)}, u32[]{:S(2)}) collective-permute-start(bf16[32,3456]{1,0:T(8,128)(2,1)S(1)} %pad_maximum_fusion.2), channel_id=1, source_target_pairs={{0,32},{8,40},{16,48},{24,56},{32,0},{40,8},{48,16},{56,24},{64,96... | collective-permute-start | bytes 663560 | tf_op jit(solution)/shard_map/ppermute | solution.py:558
  38.9 4.1 %shard_map.202.refs_5_ = f32[5,320,128]{2,1,0:T(8,128)S(1)} custom-call(bf16[64,2880]{1,0:T(8,128)(2,1)S(1)} %bitcast.28, bf16[64,2880]{1,0:T(8,128)(2,1)} %collective-permute-done.3.refs_1_, bf16[64,2880]{1,0:T(8,128)(2,1)} %collective-permute-done.1.refs_2_, bf16[64,2880]{1,0:T(8,128)(2,1)} %collective-permute-done.6.refs_3_, ...), custom_call_target="tpu_custom_call" | custom-call | tf_op jit(solution)/shard_map/pallas_call | solution.py:266
  43.2 3.2 %collective-permute-start.10 = (bf16[32,2880]{1,0:T(8,128)(2,1)S(1)}, bf16[32,2880]{1,0:T(8,128)(2,1)S(1)}, u32[]{:S(2)}, u32[]{:S(2)}) collective-permute-start(bf16[32,2880]{1,0:T(8,128)(2,1)S(1)} %slice.9), channel_id=1, source_target_pairs={{0,7},{1,0},{2,1},{3,2},{4,3},{5,4},{6,5},{7,6},{8,15},{9,8},{10,9... | collective-permute-start | bytes 552968 | tf_op jit(solution)/shard_map/ppermute | solution.py:541
  46.5 2.0 %shard_map.203.refs_6_ = f32[5,128,128]{2,1,0:T(8,128)S(1)} custom-call(bf16[64,2880]{1,0:T(8,128)(2,1)S(1)} %collective-permute-done.8.refs_0_, bf16[64,2880]{1,0:T(8,128)(2,1)S(1)} %collective-permute-done.7.refs_1_, bf16[2880,640]{1,0:T(8,128)(2,1)S(1)} %bitcast.19, f32[4,2880]{1,0:T(4,128)S(1)} %bitcast.24, f32[4,512]{1,0:T(4,128)S(1)} %bitcast.33, ...), custom_call_target="tpu_custom_call" | custom-call | tf_op jit(solution)/shard_map/pallas_call | solution.py:266
  50.0 14.0 %shard_map.204 = (bf16[32,2880]{1,0:T(8,128)(2,1)S(1)}, bf16[32,2880]{1,0:T(8,128)(2,1)S(1)}, bf16[32,2880]{1,0:T(8,128)(2,1)S(1)}, bf16[32,2880]{1,0:T(8,128)(2...) custom-call(s32[16]{0:T(128)S(1)} %bitcast.38, ...), custom_call_target="tpu_custom_call" | custom-call | tf_op jit(solution)/shard_map/pallas_call | solution.py:493
  65.0 3.1 %collective-permute-start.14 = (bf16[32,2880]{1,0:T(8,128)(2,1)S(1)}, bf16[32,2880]{1,0:T(8,128)(2,1)S(1)}, u32[]{:S(2)}, u32[]{:S(2)}) collective-permute-start(bf16[32,2880]{1,0:T(8,128)(2,1)S(1)} %get-tuple-element.85), channel_id=1, source_target_pairs={{0,7},{1,0},{2,1},{3,2},{4,3},{5,4},{6,5},{7,6},{8,15},{9,8},{10,9... | collective-permute-start | bytes 552968 | tf_op jit(solution)/shard_map/ppermute | solution.py:541
  68.0 2.0 %collective-permute-start.15 = (bf16[32,2880]{1,0:T(8,128)(2,1)S(1)}, bf16[32,2880]{1,0:T(8,128)(2,1)S(1)}, u32[]{:S(2)}, u32[]{:S(2)}) collective-permute-start(bf16[32,2880]{1,0:T(8,128)(2,1)S(1)} %get-tuple-element.87), channel_id=1, source_target_pairs={{0,7},{1,0},{2,1},{3,2},{4,3},{5,4},{6,5},{7,6},{8,15},{9,8},{10,9... | collective-permute-start | bytes 552968 | tf_op jit(solution)/shard_map/ppermute | solution.py:541
  70.0 2.3 %collective-permute-done.11 = bf16[32,2880]{1,0:T(8,128)(2,1)S(1)} collective-permute-done((bf16[32,2880]{1,0:T(8,128)(2,1)S(1)}, bf16[32,2880]{1,0:T(8,128)(2,1)S(1)}, u32[]{:S(2)}, u32[]{:S(2)}) %collective-permute-start.11) | collective-permute-done | bytes 184352 | tf_op jit(solution)/shard_map/ppermute | solution.py:538
  72.5 4.2 %collective-permute-done.15 = bf16[32,2880]{1,0:T(8,128)(2,1)S(1)} collective-permute-done((bf16[32,2880]{1,0:T(8,128)(2,1)S(1)}, bf16[32,2880]{1,0:T(8,128)(2,1)S(1)}, u32[]{:S(2)}, u32[]{:S(2)}) %collective-permute-start.15) | collective-permute-done | bytes 184352 | tf_op jit(solution)/shard_map/ppermute | solution.py:541
  76.8 2.1 %collective-permute-start.19 = (bf16[32,2880]{1,0:T(8,128)(2,1)S(1)}, bf16[32,2880]{1,0:T(8,128)(2,1)S(1)}, u32[]{:S(2)}, u32[]{:S(2)}) collective-permute-start(bf16[32,2880]{1,0:T(8,128)(2,1)S(1)} %add_convert_fusion.10), channel_id=1, source_target_pairs={{0,7},{1,0},{2,1},{3,2},{4,3},{5,4},{6,5},{7,6},{8,15},{9,8},{10,9... | collective-permute-start | bytes 552968 | tf_op jit(solution)/shard_map/ppermute | solution.py:541
  78.9 2.2 %collective-permute-start.18 = (bf16[32,2880]{1,0:T(8,128)(2,1)S(1)}, bf16[32,2880]{1,0:T(8,128)(2,1)S(1)}, u32[]{:S(2)}, u32[]{:S(2)}) collective-permute-start(bf16[32,2880]{1,0:T(8,128)(2,1)S(1)} %add_convert_fusion.9), channel_id=1, source_target_pairs={{0,7},{1,0},{2,1},{3,2},{4,3},{5,4},{6,5},{7,6},{8,15},{9,8},{10,9... | collective-permute-start | bytes 552968 | tf_op jit(solution)/shard_map/ppermute | solution.py:541
  82.8 3.0 %collective-permute-start.25 = (bf16[32,2880]{1,0:T(8,128)(2,1)S(1)}, bf16[32,2880]{1,0:T(8,128)(2,1)S(1)}, u32[]{:S(2)}, u32[]{:S(2)}) collective-permute-start(bf16[32,2880]{1,0:T(8,128)(2,1)S(1)} %add_convert_fusion.6), channel_id=1, source_target_pairs={{0,7},{1,0},{2,1},{3,2},{4,3},{5,4},{6,5},{7,6},{8,15},{9,8},{10,9... | collective-permute-start | bytes 552968 | tf_op jit(solution)/shard_map/ppermute | solution.py:541
  85.9 4.0 %collective-permute-done.17 = bf16[32,2880]{1,0:T(8,128)(2,1)S(1)} collective-permute-done((bf16[32,2880]{1,0:T(8,128)(2,1)S(1)}, bf16[32,2880]{1,0:T(8,128)(2,1)S(1)}, u32[]{:S(2)}, u32[]{:S(2)}) %collective-permute-start.17) | collective-permute-done | bytes 184352 | tf_op jit(solution)/shard_map/ppermute | solution.py:538
  90.6 3.3 %collective-permute-done.16 = bf16[32,2880]{1,0:T(8,128)(2,1)S(1)} collective-permute-done((bf16[32,2880]{1,0:T(8,128)(2,1)S(1)}, bf16[32,2880]{1,0:T(8,128)(2,1)S(1)}, u32[]{:S(2)}, u32[]{:S(2)}) %collective-permute-start.16) | collective-permute-done | bytes 184352 | tf_op jit(solution)/shard_map/ppermute | solution.py:538
  95.1 2.0 %collective-permute-start.20 = (bf16[32,2880]{1,0:T(8,128)(2,1)S(1)}, bf16[32,2880]{1,0:T(8,128)(2,1)S(1)}, u32[]{:S(2)}, u32[]{:S(2)}) collective-permute-start(bf16[32,2880]{1,0:T(8,128)(2,1)S(1)} %add_convert_fusion.3), channel_id=1, source_target_pairs={{0,1},{1,2},{2,3},{3,4},{4,5},{5,6},{6,7},{7,0},{8,9},{9,10},{10,1... | collective-permute-start | bytes 552968 | tf_op jit(solution)/shard_map/ppermute | solution.py:538
  98.4 2.2 %collective-permute-done.26 = bf16[32,2880]{1,0:T(8,128)(2,1)} collective-permute-done((bf16[32,2880]{1,0:T(8,128)(2,1)}, bf16[32,2880]{1,0:T(8,128)(2,1)}, u32[]{:S(2)}, u32[]{:S(2)}) %collective-permute-start.26) | collective-permute-done | bytes 184352 | tf_op jit(solution)/shard_map/ppermute | solution.py:541
  (107 shorter events, 19.9 us)
Async XLA Ops:
  0.6 14.3 %collective-permute-start.3 = (bf16[64,2880]{1,0:T(8,128)(2,1)}, bf16[64,2880]{1,0:T(8,128)(2,1)}, u32[]{:S(2)}, u32[]{:S(2)}) collective-permute-start(bf16[64,2880]{1,0:T(8,128)(2,1)} %bitcast.26), channel_id=1, source_target_pairs={{0,7},{1,0},{2,1},{3,2},{4,3},{5,4},{6,5},{7,6},{8,15},{9,8},{10,9... | collective-permute-start | bytes 1105928 | tf_op jit(solution)/shard_map/ppermute | solution.py:541
  6.6 11.8 %collective-permute-start.1 = (bf16[64,2880]{1,0:T(8,128)(2,1)}, bf16[64,2880]{1,0:T(8,128)(2,1)}, u32[]{:S(2)}, u32[]{:S(2)}) collective-permute-start(bf16[64,2880]{1,0:T(8,128)(2,1)} %bitcast.27), channel_id=1, source_target_pairs={{0,1},{1,2},{2,3},{3,4},{4,5},{5,6},{6,7},{7,0},{8,9},{9,10},{10,1... | collective-permute-start | bytes 1105928 | tf_op jit(solution)/shard_map/ppermute | solution.py:538
  8.7 11.7 %collective-permute-start = (bf16[8,3456]{1,0:T(8,128)(2,1)}, bf16[8,3456]{1,0:T(8,128)(2,1)S(1)}, u32[]{:S(2)}, u32[]{:S(2)}) collective-permute-start(bf16[8,3456]{1,0:T(8,128)(2,1)} %shard_map.200), channel_id=1, source_target_pairs={{0,128},{8,136},{16,144},{24,152},{32,160},{40,168},{48,176},{56,1... | collective-permute-start | bytes 165896 | tf_op jit(solution)/shard_map/ppermute | solution.py:558
  18.3 9.6 %collective-permute-start.6 = (bf16[64,2880]{1,0:T(8,128)(2,1)}, bf16[64,2880]{1,0:T(8,128)(2,1)}, u32[]{:S(2)}, u32[]{:S(2)}) collective-permute-start(bf16[64,2880]{1,0:T(8,128)(2,1)} %collective-permute-done.3.refs_1_), channel_id=1, source_target_pairs={{0,7},{1,0},{2,1},{3,2},{4,3},{5,4},{6,5},{7,6},{8,15},{9,8},{10,9... | collective-permute-start | bytes 1105928 | tf_op jit(solution)/shard_map/ppermute | solution.py:541
  18.6 10.9 %collective-permute-start.4 = (bf16[64,2880]{1,0:T(8,128)(2,1)}, bf16[64,2880]{1,0:T(8,128)(2,1)}, u32[]{:S(2)}, u32[]{:S(2)}) collective-permute-start(bf16[64,2880]{1,0:T(8,128)(2,1)} %collective-permute-done.1.refs_2_), channel_id=1, source_target_pairs={{0,1},{1,2},{2,3},{3,4},{4,5},{5,6},{6,7},{7,0},{8,9},{9,10},{10,1... | collective-permute-start | bytes 1105928 | tf_op jit(solution)/shard_map/ppermute | solution.py:538
  21.2 11.6 %collective-permute-start.2 = (bf16[16,3456]{1,0:T(8,128)(2,1)S(1)}, bf16[16,3456]{1,0:T(8,128)(2,1)}, u32[]{:S(2)}, u32[]{:S(2)}) collective-permute-start(bf16[16,3456]{1,0:T(8,128)(2,1)S(1)} %pad_maximum_fusion.3), channel_id=1, source_target_pairs={{0,64},{8,72},{16,80},{24,88},{32,96},{40,104},{48,112},{56,120},{... | collective-permute-start | bytes 331784 | tf_op jit(solution)/shard_map/ppermute | solution.py:558
  29.5 13.5 %collective-permute-start.7 = (bf16[64,2880]{1,0:T(8,128)(2,1)}, bf16[64,2880]{1,0:T(8,128)(2,1)S(1)}, u32[]{:S(2)}, u32[]{:S(2)}) collective-permute-start(bf16[64,2880]{1,0:T(8,128)(2,1)} %collective-permute-done.4.refs_4_), channel_id=1, source_target_pairs={{0,1},{1,2},{2,3},{3,4},{4,5},{5,6},{6,7},{7,0},{8,9},{9,10},{10,1... | collective-permute-start | bytes 1105928 | tf_op jit(solution)/shard_map/ppermute | solution.py:538
  29.7 13.3 %collective-permute-start.8 = (bf16[64,2880]{1,0:T(8,128)(2,1)}, bf16[64,2880]{1,0:T(8,128)(2,1)S(1)}, u32[]{:S(2)}, u32[]{:S(2)}) collective-permute-start(bf16[64,2880]{1,0:T(8,128)(2,1)} %collective-permute-done.6.refs_3_), channel_id=1, source_target_pairs={{0,7},{1,0},{2,1},{3,2},{4,3},{5,4},{6,5},{7,6},{8,15},{9,8},{10,9... | collective-permute-start | bytes 1105928 | tf_op jit(solution)/shard_map/ppermute | solution.py:541
  33.6 12.8 %collective-permute-start.5 = (bf16[32,3456]{1,0:T(8,128)(2,1)S(1)}, bf16[32,3456]{1,0:T(8,128)(2,1)S(1)}, u32[]{:S(2)}, u32[]{:S(2)}) collective-permute-start(bf16[32,3456]{1,0:T(8,128)(2,1)S(1)} %pad_maximum_fusion.2), channel_id=1, source_target_pairs={{0,32},{8,40},{16,48},{24,56},{32,0},{40,8},{48,16},{56,24},{64,96... | collective-permute-start | bytes 663560 | tf_op jit(solution)/shard_map/ppermute | solution.py:558
  43.1 6.9 %collective-permute-start.9 = (bf16[32,2880]{1,0:T(8,128)(2,1)S(1)}, bf16[32,2880]{1,0:T(8,128)(2,1)S(1)}, u32[]{:S(2)}, u32[]{:S(2)}) collective-permute-start(bf16[32,2880]{1,0:T(8,128)(2,1)S(1)} %slice.8), channel_id=1, source_target_pairs={{0,1},{1,2},{2,3},{3,4},{4,5},{5,6},{6,7},{7,0},{8,9},{9,10},{10,1... | collective-permute-start | bytes 552968 | tf_op jit(solution)/shard_map/ppermute | solution.py:538
  64.0 8.4 %collective-permute-start.11 = (bf16[32,2880]{1,0:T(8,128)(2,1)S(1)}, bf16[32,2880]{1,0:T(8,128)(2,1)S(1)}, u32[]{:S(2)}, u32[]{:S(2)}) collective-permute-start(bf16[32,2880]{1,0:T(8,128)(2,1)S(1)} %get-tuple-element.80), channel_id=1, source_target_pairs={{0,1},{1,2},{2,3},{3,4},{4,5},{5,6},{6,7},{7,0},{8,9},{9,10},{10,1... | collective-permute-start | bytes 552968 | tf_op jit(solution)/shard_map/ppermute | solution.py:538
  64.1 17.2 %collective-permute-start.22 = (bf16[64,3456]{1,0:T(8,128)(2,1)S(1)}, bf16[64,3456]{1,0:T(8,128)(2,1)S(1)}, u32[]{:S(2)}, u32[]{:S(2)}) collective-permute-start(bf16[64,3456]{1,0:T(8,128)(2,1)S(1)} %pad_maximum_fusion.1), channel_id=1, source_target_pairs={{0,16},{8,24},{16,0},{24,8},{32,48},{40,56},{48,32},{56,40},{64,80... | collective-permute-start | bytes 1327112 | tf_op jit(solution)/shard_map/ppermute | solution.py:558
  64.8 16.4 %collective-permute-start.13 = (bf16[32,2880]{1,0:T(8,128)(2,1)S(1)}, bf16[32,2880]{1,0:T(8,128)(2,1)S(1)}, u32[]{:S(2)}, u32[]{:S(2)}) collective-permute-start(bf16[32,2880]{1,0:T(8,128)(2,1)S(1)} %get-tuple-element.83), channel_id=1, source_target_pairs={{0,1},{1,2},{2,3},{3,4},{4,5},{5,6},{6,7},{7,0},{8,9},{9,10},{10,1... | collective-permute-start | bytes 552968 | tf_op jit(solution)/shard_map/ppermute | solution.py:538
  65.0 13.9 %collective-permute-start.14 = (bf16[32,2880]{1,0:T(8,128)(2,1)S(1)}, bf16[32,2880]{1,0:T(8,128)(2,1)S(1)}, u32[]{:S(2)}, u32[]{:S(2)}) collective-permute-start(bf16[32,2880]{1,0:T(8,128)(2,1)S(1)} %get-tuple-element.85), channel_id=1, source_target_pairs={{0,7},{1,0},{2,1},{3,2},{4,3},{5,4},{6,5},{7,6},{8,15},{9,8},{10,9... | collective-permute-start | bytes 552968 | tf_op jit(solution)/shard_map/ppermute | solution.py:541
  68.0 8.7 %collective-permute-start.15 = (bf16[32,2880]{1,0:T(8,128)(2,1)S(1)}, bf16[32,2880]{1,0:T(8,128)(2,1)S(1)}, u32[]{:S(2)}, u32[]{:S(2)}) collective-permute-start(bf16[32,2880]{1,0:T(8,128)(2,1)S(1)} %get-tuple-element.87), channel_id=1, source_target_pairs={{0,7},{1,0},{2,1},{3,2},{4,3},{5,4},{6,5},{7,6},{8,15},{9,8},{10,9... | collective-permute-start | bytes 552968 | tf_op jit(solution)/shard_map/ppermute | solution.py:541
  72.4 9.1 %collective-permute-start.12 = (bf16[32,2880]{1,0:T(8,128)(2,1)S(1)}, bf16[32,2880]{1,0:T(8,128)(2,1)S(1)}, u32[]{:S(2)}, u32[]{:S(2)}) collective-permute-start(bf16[32,2880]{1,0:T(8,128)(2,1)S(1)} %add_convert_fusion.11), channel_id=1, source_target_pairs={{0,1},{1,2},{2,3},{3,4},{4,5},{5,6},{6,7},{7,0},{8,9},{9,10},{10,1... | collective-permute-start | bytes 552968 | tf_op jit(solution)/shard_map/ppermute | solution.py:538
  78.9 6.9 %collective-permute-start.18 = (bf16[32,2880]{1,0:T(8,128)(2,1)S(1)}, bf16[32,2880]{1,0:T(8,128)(2,1)S(1)}, u32[]{:S(2)}, u32[]{:S(2)}) collective-permute-start(bf16[32,2880]{1,0:T(8,128)(2,1)S(1)} %add_convert_fusion.9), channel_id=1, source_target_pairs={{0,7},{1,0},{2,1},{3,2},{4,3},{5,4},{6,5},{7,6},{8,15},{9,8},{10,9... | collective-permute-start | bytes 552968 | tf_op jit(solution)/shard_map/ppermute | solution.py:541
  81.2 8.7 %collective-permute-start.17 = (bf16[32,2880]{1,0:T(8,128)(2,1)S(1)}, bf16[32,2880]{1,0:T(8,128)(2,1)S(1)}, u32[]{:S(2)}, u32[]{:S(2)}) collective-permute-start(bf16[32,2880]{1,0:T(8,128)(2,1)S(1)} %add_convert_fusion.8), channel_id=1, source_target_pairs={{0,1},{1,2},{2,3},{3,4},{4,5},{5,6},{6,7},{7,0},{8,9},{9,10},{10,1... | collective-permute-start | bytes 552968 | tf_op jit(solution)/shard_map/ppermute | solution.py:538
  81.4 15.7 %collective-permute-start.23 = (bf16[128,3456]{1,0:T(8,128)(2,1)S(1)}, bf16[128,3456]{1,0:T(8,128)(2,1)S(1)}, u32[]{:S(2)}, u32[]{:S(2)}) collective-permute-start(bf16[128,3456]{1,0:T(8,128)(2,1)S(1)} %pad_maximum_fusion.refs_1_), channel_id=1, source_target_pairs={{0,8},{8,0},{16,24},{24,16},{32,40},{40,32},{48,56},{56,48},{64,72... | collective-permute-start | bytes 2654216 | tf_op jit(solution)/shard_map/ppermute | solution.py:558
  81.6 12.3 %collective-permute-start.16 = (bf16[32,2880]{1,0:T(8,128)(2,1)S(1)}, bf16[32,2880]{1,0:T(8,128)(2,1)S(1)}, u32[]{:S(2)}, u32[]{:S(2)}) collective-permute-start(bf16[32,2880]{1,0:T(8,128)(2,1)S(1)} %add_convert_fusion.7), channel_id=1, source_target_pairs={{0,1},{1,2},{2,3},{3,4},{4,5},{5,6},{6,7},{7,0},{8,9},{9,10},{10,1... | collective-permute-start | bytes 552968 | tf_op jit(solution)/shard_map/ppermute | solution.py:538
  82.8 11.1 %collective-permute-start.25 = (bf16[32,2880]{1,0:T(8,128)(2,1)S(1)}, bf16[32,2880]{1,0:T(8,128)(2,1)S(1)}, u32[]{:S(2)}, u32[]{:S(2)}) collective-permute-start(bf16[32,2880]{1,0:T(8,128)(2,1)S(1)} %add_convert_fusion.6), channel_id=1, source_target_pairs={{0,7},{1,0},{2,1},{3,2},{4,3},{5,4},{6,5},{7,6},{8,15},{9,8},{10,9... | collective-permute-start | bytes 552968 | tf_op jit(solution)/shard_map/ppermute | solution.py:541
  90.6 7.8 %collective-permute-start.24 = (bf16[32,2880]{1,0:T(8,128)(2,1)}, bf16[32,2880]{1,0:T(8,128)(2,1)S(1)}, u32[]{:S(2)}, u32[]{:S(2)}) collective-permute-start(bf16[32,2880]{1,0:T(8,128)(2,1)} %add_convert_fusion.4), channel_id=1, source_target_pairs={{0,1},{1,2},{2,3},{3,4},{4,5},{5,6},{6,7},{7,0},{8,9},{9,10},{10,1... | collective-permute-start | bytes 552968 | tf_op jit(solution)/shard_map/ppermute | solution.py:538
  95.1 7.5 %collective-permute-start.21 = (bf16[32,2880]{1,0:T(8,128)(2,1)S(1)}, bf16[32,2880]{1,0:T(8,128)(2,1)S(1)}, u32[]{:S(2)}, u32[]{:S(2)}) collective-permute-start(bf16[32,2880]{1,0:T(8,128)(2,1)S(1)} %add_convert_fusion.5), channel_id=1, source_target_pairs={{0,7},{1,0},{2,1},{3,2},{4,3},{5,4},{6,5},{7,6},{8,15},{9,8},{10,9... | collective-permute-start | bytes 552968 | tf_op jit(solution)/shard_map/ppermute | solution.py:541
  95.1 7.4 %collective-permute-start.20 = (bf16[32,2880]{1,0:T(8,128)(2,1)S(1)}, bf16[32,2880]{1,0:T(8,128)(2,1)S(1)}, u32[]{:S(2)}, u32[]{:S(2)}) collective-permute-start(bf16[32,2880]{1,0:T(8,128)(2,1)S(1)} %add_convert_fusion.3), channel_id=1, source_target_pairs={{0,1},{1,2},{2,3},{3,4},{4,5},{5,6},{6,7},{7,0},{8,9},{9,10},{10,1... | collective-permute-start | bytes 552968 | tf_op jit(solution)/shard_map/ppermute | solution.py:538
  (24 other events, 227.0 us)
